TPU v7x, 256 devices: a whole 4x4x8 slice. The times are simulated.
256 devices in a mesh: res: 8 (over z_hi, x), dom: 32 (over z_lo, y, core).
Axes of the slice: x: 4, y: 4, z: 8 (z_hi: 2, z_lo: 4; z = z_hi * 4 + z_lo), core: 2. Of those that a mesh axis runs over, the one named last changes fastest.
Arguments:
- rhs_panel: float32 [8, 48, 8, 1024, 128], P('res', None, None, 'dom'), may hold values from -6 to 6
- inv_diag: float32 [8, 3, 3, 8, 1024, 128], P('res', None, None, None, 'dom'), may hold values from -0.04 to 0.15, as said below
- trans: float32 [8, 3, 8, 1024, 128], P('res', None, None, 'dom'), may hold values from 0.3 to 1.5
- perf_cell: int32 [8, 8192], P('res', 'dom'), may hold values from 0 to 32767
- perf_well: int32 [8, 8192], P('res', 'dom'), may hold values from 0 to 255
- perf_coef: float32 [8, 3, 8192], P('res', None, 'dom'), may hold values from -8 to 8
- perf_count: int32 [8, 32], P('res', 'dom'), may hold values from 32 to 256, as said below
- well_node: int32 [8, 256], P('res'), may hold values from 0 to 2047
- net_block: float32 [16, 2048], replicated, may hold values from -6 to 6
- net_residual: float32 [2048], replicated, may hold values from -6 to 6
Outputs:
- correction: float32 [8, 3, 8, 1024, 128], P('res', None, None, 'dom')
- schur_panel: float32 [16, 2048], replicated
Inputs may be any that keep to these rules, and one draw needn't show every extreme that they name: `perf_count`: slots below a device's count are live, the rest are ignored; in every reservoir some device has all 256 slots live. `inv_diag`: diagonal entries positive.
All inputs are finite; a program needn't handle non-finite values.
Results may differ from a plain program's by a relative error of at most 0.00015.
Values sent between devices are 32-bit elements; how exact they have to be, the bound alone decides.
A program may use at most 128 MiB of HBM per device.

v0:
```python
import math

import jax
import jax.numpy as jnp
from jax import lax
from jax.sharding import PartitionSpec as P

SWEEPS = 4


HIGH = lax.Precision.HIGHEST


def shifted(value, axis, steps):
    count = lax.axis_size(axis)
    first, last = (max(0, -steps), min(count, count - steps))
    return lax.ppermute(value, axis, [(source, source + steps) for source in range(first, last)])


def padded(block, sides, width):
    for axis, dim in sides:
        count = lax.axis_size(axis)
        forward = [(i, i + 1) for i in range(count - 1)]
        backward = [(target, source) for source, target in forward]
        low = lax.ppermute(
            lax.slice_in_dim(block, block.shape[dim] - width, None, axis=dim), axis, forward
        )
        high = lax.ppermute(lax.slice_in_dim(block, 0, width, axis=dim), axis, backward)
        block = jnp.concatenate([low, block, high], axis=dim)
    return block


def copy_for_each(shard, axis):
    copies = jnp.broadcast_to(shard, (lax.axis_size(axis), *shard.shape))
    return lax.all_to_all(copies, axis, split_axis=0, concat_axis=0, tiled=True)


def over_copies(shard, axis):
    everything = copy_for_each(shard, axis)
    return jnp.sum(everything, axis=0)


def apply_inverse(inverse, panel_now):
    pieces = panel_now.reshape((3, -1) + panel_now.shape[1:])
    result = []
    for comp in range(3):
        result.append(
            inverse[comp, 0][None] * pieces[0]
            + inverse[comp, 1][None] * pieces[1]
            + inverse[comp, 2][None] * pieces[2]
        )
    return jnp.stack(result).reshape(panel_now.shape)


def coupled(panel_now, x_padded, face_x, face_x_next, face_y, face_z):
    face_y_next = jnp.pad(face_y[:, :, 1:], ((0, 0), (0, 0), (0, 1)))
    face_z_next = jnp.pad(face_z[1:], ((0, 1), (0, 0), (0, 0)))
    y_padded = jnp.pad(panel_now, ((0, 0), (0, 0), (0, 0), (1, 1)))
    z_padded = jnp.pad(panel_now, ((0, 0), (1, 1), (0, 0), (0, 0)))
    summed = face_x * x_padded[:, :, :-2] + face_x_next * x_padded[:, :, 2:]
    summed = summed + face_y * y_padded[..., :-2] + face_y_next * y_padded[..., 2:]
    summed = summed + face_z * z_padded[:, :-2] + face_z_next * z_padded[:, 2:]
    return summed


def local(
    rhs_panel,
    inv_diag,
    trans,
    perf_cell,
    perf_well,
    perf_coef,
    perf_count,
    well_node,
    net_block,
    net_residual,
):
    source = rhs_panel[0]
    inverse = inv_diag[0]
    face_x = trans[0, 0]
    face_y = trans[0, 1]
    face_z = trans[0, 2]
    edge_coeff = shifted(face_x[:, :1, :], "dom", -1)
    face_x_next = jnp.concatenate([face_x[:, 1:, :], edge_coeff], axis=1)
    panel_now = apply_inverse(inverse, source)
    for sweep_index in range(SWEEPS):
        x_padded = padded(panel_now, (("dom", 2),), 1)
        panel_now = apply_inverse(
            inverse, source + coupled(panel_now, x_padded, face_x, face_x_next, face_y, face_z)
        )
    cols = source.shape[0] // 3
    perf_slots = perf_cell.shape[1]
    wells = well_node.shape[1]
    nodes = net_block.shape[1]
    picked = jnp.take(panel_now.reshape(3 * cols, -1), perf_cell[0], axis=1).reshape(
        3, cols, perf_slots
    )
    coeffs = perf_coef[0]
    weighted = (
        coeffs[0][None] * picked[0] + coeffs[1][None] * picked[1] + coeffs[2][None] * picked[2]
    )
    live_slots = lax.iota(jnp.int32, perf_slots) < perf_count[0, 0]
    well_onehot = jnp.where(
        (perf_well[0][:, None] == lax.iota(jnp.int32, wells)[None, :]) & live_slots[:, None],
        1.0,
        0.0,
    ).astype(jnp.float32)
    well_rows = jnp.dot(weighted, well_onehot, precision=HIGH)
    node_onehot = jnp.where(
        well_node[0][:, None] == lax.iota(jnp.int32, nodes)[None, :], 1.0, 0.0
    ).astype(jnp.float32)
    group_rows = over_copies(well_rows, "dom")
    coupling = over_copies(jnp.dot(group_rows, node_onehot, precision=HIGH), "res")
    schur_panel = net_block - coupling
    weights = jnp.dot(schur_panel, net_residual, precision=HIGH) / math.sqrt(nodes)
    field = jnp.einsum(
        "ajlcy,j->alcy", panel_now.reshape((3, cols) + panel_now.shape[1:]), weights, precision=HIGH
    )
    return (field[None], schur_panel)


def solution(mesh):
    return jax.shard_map(
        local,
        mesh=mesh,
        in_specs=(
            P("res", None, None, "dom", None),
            P("res", None, None, None, "dom", None),
            P("res", None, None, "dom", None),
            P("res", "dom"),
            P("res", "dom"),
            P("res", None, "dom"),
            P("res", "dom"),
            P("res", None),
            P(),
            P(),
        ),
        out_specs=(P("res", None, None, "dom", None), P()),
        check_vma=False,
    )
```

profile of v0, /device:TPU:32, one launch (start us, length us, event | category | flops | bytes accessed | tf_op | source)
XLA Modules:
  0.0 204.4 jit_solution(9736865773356439376)
XLA Ops:
  2.1 4.1 %multiply_add_fusion.2 = (f32[1,16,8,32,128]{4,3,2,1,0:T(8,128)S(1)}, f32[1,16,8,32,128]{4,3,2,1,0:T(8,128)S(1)}, f32[1,16,8,32,128]{4,3,2,1,0:T(8,128)S(1)}) fusion(f32[1,48,8,32,128]{4,3,2,1,0:T(8,128)} %param.10, f32[8,32,128]{2,1,0:T(8,128)S(1)} %get-tuple-element.32, f32[8,32,128]{2,1,0:T(8,128)S(1)} %get-tuple-element.33, ...), kind=kLoop, calls=%fused_computation.97 | loop fusion | flops 7864320 | bytes 13762560 | tf_op jit(solution)/shard_map/add | solution.py:48
  7.3 2.2 %collective-permute-start = (f32[48,8,1,128]{3,2,1,0:T(1,128)S(1)}, f32[48,8,1,128]{3,2,1,0:T(1,128)S(1)}, u32[]{:S(2)}, u32[]{:S(2)}) collective-permute-start(f32[48,8,1,128]{3,2,1,0:T(1,128)S(1)} %get-tuple-element.20), channel_id=1, source_target_pairs={{0,1},{1,2},{2,3},{3,4},{4,5},{5,6},{6,7},{7,8},{8,9},{9,10},{10,1... | collective-permute-start | bytes 589832 | tf_op jit(solution)/shard_map/ppermute | solution.py:25
  9.5 5.8 %collective-permute-start.2 = (f32[48,8,1,128]{3,2,1,0:T(1,128)S(1)}, f32[48,8,1,128]{3,2,1,0:T(1,128)S(1)}, u32[]{:S(2)}, u32[]{:S(2)}) collective-permute-start(f32[48,8,1,128]{3,2,1,0:T(1,128)S(1)} %get-tuple-element.21), channel_id=1, source_target_pairs={{1,0},{2,1},{3,2},{4,3},{5,4},{6,5},{7,6},{8,7},{9,8},{10,9},{11,1... | collective-permute-start | bytes 589832 | tf_op jit(solution)/shard_map/ppermute | solution.py:28
  15.3 1.9 collective-permute-start.1
  18.6 7.0 %fusion.3 = f32[48,8,32,128]{3,2,1,0:T(8,128)} fusion(f32[48,8,32,128]{3,2,1,0:T(8,128)S(1)} %bitcast.97, f32[48,8,1,128]{3,2,1,0:T(1,128)S(1)} %collective-permute-done.2, f32[48,8,1,128]{3,2,1,0:T(1,128)S(1)} %collective-permute-done, f32[1,48,8,32,128]{4,3,2,1,0:T(8,128)S(1)} %bitcast.95, f32[8,32,128]{2,1,0:T(8,128)S(1)} %pad.43, ...), kind=kLoop, calls=%fused_computation.20 | loop fusion | flops 22020096 | bytes 20054016 | tf_op jit(solution)/shard_map/add | solution.py:89
  25.6 4.0 %add_bitcast_fusion.11 = (f32[1,16,8,32,128]{4,3,2,1,0:T(8,128)S(1)}, f32[1,16,8,32,128]{4,3,2,1,0:T(8,128)S(1)}, f32[1,16,8,32,128]{4,3,2,1,0:T(8,128)S(1)}) fusion(f32[48,8,32,128]{3,2,1,0:T(8,128)} %fusion.3, f32[8,32,128]{2,1,0:T(8,128)S(1)} %get-tuple-element.32, f32[8,32,128]{2,1,0:T(8,128)S(1)} %get-tuple-element.33, ...), kind=kLoop, calls=%fused_computation.94 | loop fusion | flops 7864320 | bytes 13762560 | tf_op jit(solution)/shard_map/stack | solution.py:52
  30.8 2.0 collective-permute-start.3
  32.8 5.8 %collective-permute-start.4 = (f32[48,8,1,128]{3,2,1,0:T(1,128)S(1)}, f32[48,8,1,128]{3,2,1,0:T(1,128)S(1)}, u32[]{:S(2)}, u32[]{:S(2)}) collective-permute-start(f32[48,8,1,128]{3,2,1,0:T(1,128)S(1)} %get-tuple-element.16), channel_id=1, source_target_pairs={{1,0},{2,1},{3,2},{4,3},{5,4},{6,5},{7,6},{8,7},{9,8},{10,9},{11,1... | collective-permute-start | bytes 589832 | tf_op jit(solution)/shard_map/ppermute | solution.py:28
  41.8 7.0 %fusion.8 = f32[48,8,32,128]{3,2,1,0:T(8,128)} fusion(f32[48,8,32,128]{3,2,1,0:T(8,128)S(1)} %bitcast.101, f32[48,8,1,128]{3,2,1,0:T(1,128)S(1)} %collective-permute-done.4, f32[48,8,1,128]{3,2,1,0:T(1,128)S(1)} %collective-permute-done.3, f32[1,48,8,32,128]{4,3,2,1,0:T(8,128)S(1)} %bitcast.95, f32[8,32,128]{2,1,0:T(8,128)S(1)} %pad.43, ...), kind=kLoop, calls=%fused_computation.25 | loop fusion | flops 22020096 | bytes 20054016 | tf_op jit(solution)/shard_map/add | solution.py:89
  48.8 4.0 %add_bitcast_fusion.8 = (f32[1,16,8,32,128]{4,3,2,1,0:T(8,128)S(1)}, f32[1,16,8,32,128]{4,3,2,1,0:T(8,128)S(1)}, f32[1,16,8,32,128]{4,3,2,1,0:T(8,128)S(1)}) fusion(f32[48,8,32,128]{3,2,1,0:T(8,128)} %fusion.8, f32[8,32,128]{2,1,0:T(8,128)S(1)} %get-tuple-element.32, f32[8,32,128]{2,1,0:T(8,128)S(1)} %get-tuple-element.33, ...), kind=kLoop, calls=%fused_computation.91 | loop fusion | flops 7864320 | bytes 13762560 | tf_op jit(solution)/shard_map/stack | solution.py:52
  54.0 1.9 collective-permute-start.5
  55.9 6.1 %collective-permute-start.6 = (f32[48,8,1,128]{3,2,1,0:T(1,128)S(1)}, f32[48,8,1,128]{3,2,1,0:T(1,128)S(1)}, u32[]{:S(2)}, u32[]{:S(2)}) collective-permute-start(f32[48,8,1,128]{3,2,1,0:T(1,128)S(1)} %get-tuple-element.11), channel_id=1, source_target_pairs={{1,0},{2,1},{3,2},{4,3},{5,4},{6,5},{7,6},{8,7},{9,8},{10,9},{11,1... | collective-permute-start | bytes 589832 | tf_op jit(solution)/shard_map/ppermute | solution.py:28
  65.0 7.0 %fusion.13 = f32[48,8,32,128]{3,2,1,0:T(8,128)} fusion(f32[48,8,32,128]{3,2,1,0:T(8,128)S(1)} %bitcast.103, f32[48,8,1,128]{3,2,1,0:T(1,128)S(1)} %collective-permute-done.6, f32[48,8,1,128]{3,2,1,0:T(1,128)S(1)} %collective-permute-done.5, f32[1,48,8,32,128]{4,3,2,1,0:T(8,128)S(1)} %bitcast.95, f32[8,32,128]{2,1,0:T(8,128)S(1)} %pad.43, ...), kind=kLoop, calls=%fused_computation.30 | loop fusion | flops 22020096 | bytes 20054016 | tf_op jit(solution)/shard_map/add | solution.py:89
  72.0 4.0 %add_bitcast_fusion.5 = (f32[1,16,8,32,128]{4,3,2,1,0:T(8,128)S(1)}, f32[1,16,8,32,128]{4,3,2,1,0:T(8,128)S(1)}, f32[1,16,8,32,128]{4,3,2,1,0:T(8,128)S(1)}) fusion(f32[48,8,32,128]{3,2,1,0:T(8,128)} %fusion.13, f32[8,32,128]{2,1,0:T(8,128)S(1)} %get-tuple-element.32, f32[8,32,128]{2,1,0:T(8,128)S(1)} %get-tuple-element.33, ...), kind=kLoop, calls=%fused_computation.88 | loop fusion | flops 7864320 | bytes 13762560 | tf_op jit(solution)/shard_map/stack | solution.py:52
  79.1 5.9 %collective-permute-start.8 = (f32[48,8,1,128]{3,2,1,0:T(1,128)S(1)}, f32[48,8,1,128]{3,2,1,0:T(1,128)S(1)}, u32[]{:S(2)}, u32[]{:S(2)}) collective-permute-start(f32[48,8,1,128]{3,2,1,0:T(1,128)S(1)} %get-tuple-element.6), channel_id=1, source_target_pairs={{1,0},{2,1},{3,2},{4,3},{5,4},{6,5},{7,6},{8,7},{9,8},{10,9},{11,1... | collective-permute-start | bytes 589832 | tf_op jit(solution)/shard_map/ppermute | solution.py:28
  88.2 7.0 %fusion.18 = f32[48,8,32,128]{3,2,1,0:T(8,128)} fusion(f32[48,8,32,128]{3,2,1,0:T(8,128)S(1)} %bitcast.99, f32[48,8,1,128]{3,2,1,0:T(1,128)S(1)} %collective-permute-done.8, f32[48,8,1,128]{3,2,1,0:T(1,128)S(1)} %collective-permute-done.7, f32[1,48,8,32,128]{4,3,2,1,0:T(8,128)S(1)} %bitcast.95, f32[8,32,128]{2,1,0:T(8,128)S(1)} %pad.43, ...), kind=kLoop, calls=%fused_computation.35 | loop fusion | flops 22020096 | bytes 20054016 | tf_op jit(solution)/shard_map/add | solution.py:89
  95.2 4.2 %add_bitcast_fusion.2 = (f32[1,16,8,32,128]{4,3,2,1,0:T(8,128)S(1)}, f32[1,16,8,32,128]{4,3,2,1,0:T(8,128)S(1)}, f32[1,16,8,32,128]{4,3,2,1,0:T(8,128)S(1)}) fusion(f32[48,8,32,128]{3,2,1,0:T(8,128)} %fusion.18, f32[8,32,128]{2,1,0:T(8,128)S(1)} %get-tuple-element.32, f32[8,32,128]{2,1,0:T(8,128)S(1)} %get-tuple-element.33, ...), kind=kLoop, calls=%fused_computation.85 | loop fusion | flops 7864320 | bytes 13762560 | tf_op jit(solution)/shard_map/stack | solution.py:52
  99.4 3.9 %pad_maximum_fusion.12 = f32[3,16,8,32,128]{4,3,2,1,0:T(8,128)} fusion(f32[1,16,8,32,128]{4,3,2,1,0:T(8,128)S(1)} %get-tuple-element.4, f32[1,16,8,32,128]{4,3,2,1,0:T(8,128)S(1)} %get-tuple-element.3, f32[1,16,8,32,128]{4,3,2,1,0:T(8,128)S(1)} %get-tuple-element.2), kind=kLoop, calls=%fused_computation.77 | loop fusion | flops 3145728 | bytes 12582912 | tf_op jit(solution)/shard_map/stack | solution.py:52
  103.3 7.2 %reshape_reshape.3 = f32[48,32768]{1,0:T(8,128)} reshape(f32[3,16,8,32,128]{4,3,2,1,0:T(8,128)} %pad_maximum_fusion.12) | data formatting | bytes 12582912 | tf_op jit(solution)/shard_map/reshape;reshape | solution.py:95
  110.5 11.4 %copy.14 = f32[48,32768]{0,1:T(8,128)} copy(f32[48,32768]{1,0:T(8,128)} %reshape_reshape.3) | data formatting | bytes 12582912 | tf_op jit(solution)/shard_map/reshape;reshape | solution.py:95
  122.0 6.5 %gather_fusion = f32[256,48]{1,0:T(8,128)S(1)} fusion(f32[48,32768]{0,1:T(8,128)} %copy.14, s32[1024]{0:T(1024)S(1)} %pad_clamp_fusion), kind=kCustom, calls=%fused_computation | custom fusion | bytes 99328 | tf_op jit(solution)/shard_map/jit(_take)/gather | solution.py:95
  129.3 23.9 %all_to_all.10 = f32[32,16,256]{2,1,0:T(8,128)S(1)} all-to-all(f32[32,16,256]{2,1,0:T(8,128)S(1)} %broadcast_in_dim.54), channel_id=1, replica_groups=mesh['res'=8,'dom'=32] {'dom'}, dimensions={0} | all-to-all | bytes 1048576 | tf_op jit(solution)/shard_map/all_to_all | solution.py:35
  154.7 39.2 %all_to_all.11 = f32[8,16,2048]{2,1,0:T(8,128)S(1)} all-to-all(f32[8,16,2048]{2,1,0:T(8,128)S(1)} %broadcast_in_dim.57), channel_id=1, replica_groups=mesh['res'=8,'dom'=32] {'res'}, dimensions={0} | all-to-all | bytes 2097152 | tf_op jit(solution)/shard_map/all_to_all | solution.py:35
  194.2 10.2 %fusion.48 = f32[1,3,8,32,128]{4,0,3,2,1:T(1,128)} fusion(f32[16,1,1,1,1]{0,1,4,3,2:T(1,128)S(1)} %fusion.53, f32[3,16,8,32,128]{4,3,2,1,0:T(8,128)} %pad_maximum_fusion.12), kind=kOutput, calls=%fused_computation.78 | convolution fusion | flops 18874368 | bytes 6684736 | tf_op jit(solution)/shard_map/ajlcy,j->alcy/dot_general | solution.py:116
  (62 shorter events, 20.5 us)
Async XLA Ops:
  0.6 193.3 %copy-start = (f32[2048]{0:T(1024)S(1)}, f32[2048]{0:T(1024)}, u32[]{:S(2)}) copy-start(f32[2048]{0:T(1024)} %param.19) | copy-start | bytes 24580
  6.1 12.5 %slice-start = ((s8[6291456]{0:T(1024)(128)(4,1)}), s8[4194304]{0:T(1024)(128)(4,1)S(1)}, s32[]{:S(2)}) async-start(s8[6291456]{0:T(1024)(128)(4,1)} %bitcast.94), calls=%async_computation.2 | async-start | bytes 8388608
  6.1 9.2 %copy-start.1 = (f32[1,3,8,32,128]{4,3,2,1,0:T(8,128)S(1)}, f32[1,3,8,32,128]{4,3,2,1,0:T(8,128)}, u32[]{:S(2)}) copy-start(f32[1,3,8,32,128]{4,3,2,1,0:T(8,128)} %param.12) | copy-start | bytes 1179652
  6.1 11.1 %copy-start.5 = (s32[1,256]{1,0:T(1,128)S(1)}, s32[1,256]{1,0:T(1,128)}, u32[]{:S(2)}) copy-start(s32[1,256]{1,0:T(1,128)} %param.13) | copy-start | bytes 3076
  6.2 12.5 %slice-start.1 = ((s8[6291456]{0:T(1024)(128)(4,1)}), s8[2097152]{0:T(1024)(128)(4,1)S(1)}, s32[]{:S(2)}) async-start(s8[6291456]{0:T(1024)(128)(4,1)} %bitcast.94), calls=%async_computation.3 | async-start | bytes 4194304
  7.3 11.3 %collective-permute-start = (f32[48,8,1,128]{3,2,1,0:T(1,128)S(1)}, f32[48,8,1,128]{3,2,1,0:T(1,128)S(1)}, u32[]{:S(2)}, u32[]{:S(2)}) collective-permute-start(f32[48,8,1,128]{3,2,1,0:T(1,128)S(1)} %get-tuple-element.20), channel_id=1, source_target_pairs={{0,1},{1,2},{2,3},{3,4},{4,5},{5,6},{6,7},{7,8},{8,9},{9,10},{10,1... | collective-permute-start | bytes 589832 | tf_op jit(solution)/shard_map/ppermute | solution.py:25
  9.5 9.1 %collective-permute-start.2 = (f32[48,8,1,128]{3,2,1,0:T(1,128)S(1)}, f32[48,8,1,128]{3,2,1,0:T(1,128)S(1)}, u32[]{:S(2)}, u32[]{:S(2)}) collective-permute-start(f32[48,8,1,128]{3,2,1,0:T(1,128)S(1)} %get-tuple-element.21), channel_id=1, source_target_pairs={{1,0},{2,1},{3,2},{4,3},{5,4},{6,5},{7,6},{8,7},{9,8},{10,9},{11,1... | collective-permute-start | bytes 589832 | tf_op jit(solution)/shard_map/ppermute | solution.py:28
  15.3 3.2 %collective-permute-start.1 = (f32[8,1,128]{2,1,0:T(1,128)S(1)}, f32[8,1,128]{2,1,0:T(1,128)S(1)}, u32[]{:S(2)}, u32[]{:S(2)}) collective-permute-start(f32[8,1,128]{2,1,0:T(1,128)S(1)} %slice.395), channel_id=1, source_target_pairs={{1,0},{2,1},{3,2},{4,3},{5,4},{6,5},{7,6},{8,7},{9,8},{10,9},{11,1... | collective-permute-start | bytes 12296 | tf_op jit(solution)/shard_map/ppermute | solution.py:17
  30.8 9.2 %collective-permute-start.3 = (f32[48,8,1,128]{3,2,1,0:T(1,128)S(1)}, f32[48,8,1,128]{3,2,1,0:T(1,128)S(1)}, u32[]{:S(2)}, u32[]{:S(2)}) collective-permute-start(f32[48,8,1,128]{3,2,1,0:T(1,128)S(1)} %get-tuple-element.15), channel_id=1, source_target_pairs={{0,1},{1,2},{2,3},{3,4},{4,5},{5,6},{6,7},{7,8},{8,9},{9,10},{10,1... | collective-permute-start | bytes 589832 | tf_op jit(solution)/shard_map/ppermute | solution.py:25
  32.8 9.0 %collective-permute-start.4 = (f32[48,8,1,128]{3,2,1,0:T(1,128)S(1)}, f32[48,8,1,128]{3,2,1,0:T(1,128)S(1)}, u32[]{:S(2)}, u32[]{:S(2)}) collective-permute-start(f32[48,8,1,128]{3,2,1,0:T(1,128)S(1)} %get-tuple-element.16), channel_id=1, source_target_pairs={{1,0},{2,1},{3,2},{4,3},{5,4},{6,5},{7,6},{8,7},{9,8},{10,9},{11,1... | collective-permute-start | bytes 589832 | tf_op jit(solution)/shard_map/ppermute | solution.py:28
  52.8 9.2 %copy-start.4 = (f32[1,3,256]{2,0,1:T(1,128)S(1)}, f32[1,3,256]{2,0,1:T(1,128)}, u32[]{:S(2)}) copy-start(f32[1,3,256]{2,0,1:T(1,128)} %param.15) | copy-start | bytes 9220
  54.0 9.3 %collective-permute-start.5 = (f32[48,8,1,128]{3,2,1,0:T(1,128)S(1)}, f32[48,8,1,128]{3,2,1,0:T(1,128)S(1)}, u32[]{:S(2)}, u32[]{:S(2)}) collective-permute-start(f32[48,8,1,128]{3,2,1,0:T(1,128)S(1)} %get-tuple-element.10), channel_id=1, source_target_pairs={{0,1},{1,2},{2,3},{3,4},{4,5},{5,6},{6,7},{7,8},{8,9},{9,10},{10,1... | collective-permute-start | bytes 589832 | tf_op jit(solution)/shard_map/ppermute | solution.py:25
  55.9 9.1 %collective-permute-start.6 = (f32[48,8,1,128]{3,2,1,0:T(1,128)S(1)}, f32[48,8,1,128]{3,2,1,0:T(1,128)S(1)}, u32[]{:S(2)}, u32[]{:S(2)}) collective-permute-start(f32[48,8,1,128]{3,2,1,0:T(1,128)S(1)} %get-tuple-element.11), channel_id=1, source_target_pairs={{1,0},{2,1},{3,2},{4,3},{5,4},{6,5},{7,6},{8,7},{9,8},{10,9},{11,1... | collective-permute-start | bytes 589832 | tf_op jit(solution)/shard_map/ppermute | solution.py:28
  77.2 9.3 %collective-permute-start.7 = (f32[48,8,1,128]{3,2,1,0:T(1,128)S(1)}, f32[48,8,1,128]{3,2,1,0:T(1,128)S(1)}, u32[]{:S(2)}, u32[]{:S(2)}) collective-permute-start(f32[48,8,1,128]{3,2,1,0:T(1,128)S(1)} %get-tuple-element.5), channel_id=1, source_target_pairs={{0,1},{1,2},{2,3},{3,4},{4,5},{5,6},{6,7},{7,8},{8,9},{9,10},{10,1... | collective-permute-start | bytes 589832 | tf_op jit(solution)/shard_map/ppermute | solution.py:25
  79.1 9.1 %collective-permute-start.8 = (f32[48,8,1,128]{3,2,1,0:T(1,128)S(1)}, f32[48,8,1,128]{3,2,1,0:T(1,128)S(1)}, u32[]{:S(2)}, u32[]{:S(2)}) collective-permute-start(f32[48,8,1,128]{3,2,1,0:T(1,128)S(1)} %get-tuple-element.6), channel_id=1, source_target_pairs={{1,0},{2,1},{3,2},{4,3},{5,4},{6,5},{7,6},{8,7},{9,8},{10,9},{11,1... | collective-permute-start | bytes 589832 | tf_op jit(solution)/shard_map/ppermute | solution.py:28
  110.5 18.1 %copy-start.6 = (s32[1,256]{1,0:T(1,128)S(1)}, s32[1,256]{1,0:T(1,128)}, u32[]{:S(2)}) copy-start(s32[1,256]{1,0:T(1,128)} %param.14) | copy-start | bytes 3076
  110.5 42.7 %copy-start.7 = (s32[1,256]{1,0:T(1,128)S(1)}, s32[1,256]{1,0:T(1,128)}, u32[]{:S(2)}) copy-start(s32[1,256]{1,0:T(1,128)} %param.17) | copy-start | bytes 3076
  121.9 72.0 %copy-start.3 = (f32[16,2048]{1,0:T(8,128)S(1)}, f32[16,2048]{1,0:T(8,128)}, u32[]{:S(2)}) copy-start(f32[16,2048]{1,0:T(8,128)} %param.18) | copy-start | bytes 393220
  194.0 10.5 %copy-start.2 = (f32[16,2048]{1,0:T(8,128)}, f32[16,2048]{1,0:T(8,128)S(1)}, u32[]{:S(2)}) copy-start(f32[16,2048]{1,0:T(8,128)S(1)} %sub.3) | copy-start | bytes 393220
where the time goes:
time: 205 us; the launch traced here: 204 us
  blocking collectives  63.1 us (31%)
  other arithmetic  56 us (27%)
  starting transfers between devices  33.5 us (16%)
  local copies, waits for them, and re-layouts  28.1 us (14%)
  matrix products  12.4 us (6%)
  waiting for transfers between devices  9.72 us (5%)
    all_to_all x2, blocking collectives, copy_for_each(): return lax.all_to_all(copies, axis, split_axis=0, concat_axis=0, tiled=True)  63.1 us
    add x4, other arithmetic, local(): source + coupled(panel_now, x_padded, face_x, face_x_next, face_y, face_z)  27.9 us
    another operation x9, other arithmetic, apply_inverse(): return jnp.stack(result).reshape(panel_now.shape)  23.8 us
    ppermute x4, starting transfers between devices, padded(): lax.ppermute(lax.slice_in_dim(block, 0, width, axis=dim), axis, backward)  23.6 us
    another operation x2, local copies, waits for them, and re-layouts, local(): panel_now.reshape(3 * cols, -1)  18.6 us
    dot_general x1, matrix products, local(): jnp.einsum('ajlcy,j->alcy', panel_now.reshape((3, cols) + panel_now.shape...  10.2 us
    ppermute x4, starting transfers between devices, padded(): lax.ppermute(lax.slice_in_dim(block, block.shape[dim] - width, None, axis...  7.99 us
    gather x1, local copies, waits for them, and re-layouts, local(): jnp.take(panel_now.reshape(3 * cols, -1), perf_cell[0], axis=1)  6.53 us
  transfers between devices with their start and end apart: 9, of which 7 were waited for; matrix products, arithmetic and copies ran while one was open for 0% of the time, Pallas kernels for 0%

commit v1 on v0

v1 whole, which is shorter than its diff:
```python
import functools
import math

import jax
import jax.numpy as jnp
from jax import lax
from jax.experimental import pallas as pl
from jax.experimental.pallas import tpu as pltpu
from jax.sharding import PartitionSpec as P

MESH = pl.DeviceIdType.MESH
SWEEPS = 4
COLS, LZ, CX, NY, NET, WELLS, SLOTS = 16, 8, 32, 128, 2048, 256, 256
RES, DOM = 8, 32
GROUPS = 4
GC = COLS // GROUPS
LOW, FIRST, LAST, HIGH = 7, 8, 39, 40
ROWS = 48
BLOCKS = COLS * 3 * LZ
GB = BLOCKS // GROUPS
PIECES = 3


def kernel(
    rhs, inv, trans, cell, well, coef, count, node, net, resid,
    corr_out, schur_out,
    q0, qa, qb, inv_v, trans_v, scale, edge, txm, txp, tym, typ, mats,
    cell_s, well_s, coef_s, count_s, nodes, net_v, resid_v,
    rows, parts, every, hot, lhs, wcol, corr_v,
    in_sem, rhs_sem, halo_send, halo_recv, edge_send, edge_recv,
    node_send, node_recv, rs_send, rs_recv, ga_send, ga_recv, gb_send, gb_recv, out_sem,
):
    f32 = jnp.float32
    res, dom = lax.axis_index("res"), lax.axis_index("dom")
    zlo, yc = dom // 8, dom % 8
    has_left, has_right = dom > 0, dom < DOM - 1

    def local(src, dst, i):
        return pltpu.make_async_copy(src, dst, in_sem.at[i])

    c_trans = local(trans, trans_v, 0)
    c_inv = local(inv, inv_v, 1)
    c_node = local(node, nodes.at[pl.ds(res, 1)], 2)
    c_small = [
        local(cell, cell_s, 3),
        local(well, well_s, 4),
        local(coef, coef_s, 5),
        local(count, count_s, 6),
        local(net, net_v, 7),
        local(resid, resid_v, 8),
    ]
    c_trans.start()
    c_node.start()
    c_inv.start()

    @pl.loop(0, COLS)
    def _(j):
        for c in range(3):
            pltpu.make_async_copy(
                rhs.at[pl.ds((c * COLS + j) * LZ, LZ)],
                q0.at[pl.ds((j * 3 + c) * LZ, LZ), pl.ds(FIRST, CX), :],
                rhs_sem.at[j // GC],
            ).start()

    for copy in c_small:
        copy.start()

    barrier = pltpu.get_barrier_semaphore()

    @pl.loop(1, DOM)
    def _(i):
        pl.semaphore_signal(
            barrier, inc=1, device_id={"dom": lax.rem(dom + i, DOM)}, device_id_type=MESH
        )

    def peer_a(i):
        there = lax.rem(res * 4 + zlo + i, 32)
        return there // 4, lax.rem(there, 4) * 8 + yc

    @pl.loop(1, RES)
    def _(i):
        for z in range(4):
            pl.semaphore_signal(
                barrier,
                inc=1,
                device_id={"res": lax.rem(res + i, RES), "dom": z * 8 + yc},
                device_id_type=MESH,
            )

    lane = lax.broadcasted_iota(jnp.int32, (8, NY), 1)

    c_trans.wait()

    @pl.loop(0, CX // 8)
    def _(xt):
        at = pl.ds(xt * 8, 8)
        own = pl.ds(xt * 8 + FIRST, 8)
        e = jnp.ones((8, NY), f32)
        for l in range(LZ):
            if l:
                e = 1.0 / (trans_v[16 + l, at, :] * e)
            scale[l, own, :] = e
            edge[l, own, :] = trans_v[l, at, :] * e
            ty = trans_v[8 + l, at, :]
            tym[l, at, :] = jnp.where(lane == 0, 0.0, ty * e * pltpu.roll(e, 1, axis=1))
            typ[l, at, :] = jnp.where(lane == NY - 1, 0.0, e * pltpu.roll(ty * e, NY - 1, axis=1))

    @pl.when(jnp.logical_not(has_left))
    def _():
        scale[:, LOW : LOW + 1, :] = jnp.zeros((LZ, 1, NY), f32)
        for buf in (q0, qa, qb):

            @pl.loop(0, BLOCKS)
            def _(b):
                buf[b, LOW : LOW + 1, :] = jnp.zeros((1, NY), f32)

    @pl.when(jnp.logical_not(has_right))
    def _():
        edge[:, HIGH : HIGH + 1, :] = jnp.zeros((LZ, 1, NY), f32)
        for buf in (q0, qa, qb):

            @pl.loop(0, BLOCKS)
            def _(b):
                buf[b, HIGH : HIGH + 1, :] = jnp.zeros((1, NY), f32)

    c_node.wait()
    pl.semaphore_wait(barrier, DOM - 1 + 4 * (RES - 1))

    def remote(src, dst, send, recv, **where):
        return pltpu.make_async_remote_copy(
            src_ref=src, dst_ref=dst, send_sem=send, recv_sem=recv, device_id=where,
            device_id_type=MESH,
        )

    to_right = remote(
        scale.at[:, LAST, :], scale.at[:, LOW, :], edge_send.at[0], edge_recv.at[0],
        dom=jnp.minimum(dom + 1, DOM - 1),
    )
    to_left = remote(
        edge.at[:, FIRST, :], edge.at[:, HIGH, :], edge_send.at[1], edge_recv.at[1],
        dom=jnp.maximum(dom - 1, 0),
    )
    pl.when(has_right)(to_right.start)
    pl.when(has_left)(to_left.start)

    def node_copy(i):
        return remote(
            nodes.at[pl.ds(res, 1)], nodes.at[pl.ds(res, 1)], node_send.at[i], node_recv.at[i],
            res=lax.rem(res + i, RES),
        )

    @pl.loop(1, RES)
    def _(i):
        node_copy(i).start()

    def halo(buf, k, g, side):
        at = pl.ds(g * GB, GB)
        if side == 0:
            return remote(
                buf.at[at, LAST, :], buf.at[at, LOW, :], halo_send.at[k, g, 0],
                halo_recv.at[k, g, 0], dom=jnp.minimum(dom + 1, DOM - 1),
            )
        return remote(
            buf.at[at, FIRST, :], buf.at[at, HIGH, :], halo_send.at[k, g, 1],
            halo_recv.at[k, g, 1], dom=jnp.maximum(dom - 1, 0),
        )

    def halo_start(buf, k, g):
        pl.when(has_right)(halo(buf, k, g, 0).start)
        pl.when(has_left)(halo(buf, k, g, 1).start)

    def halo_wait(buf, k, g):
        @pl.when(has_right)
        def _():
            halo(buf, k, g, 0).wait_send()
            halo(buf, k, g, 1).wait_recv()

        @pl.when(has_left)
        def _():
            halo(buf, k, g, 1).wait_send()
            halo(buf, k, g, 0).wait_recv()

    c_inv.wait()

    @pl.loop(0, GROUPS)
    def _(g):
        whole = q0.at[pl.ds(g * GB, GB), pl.ds(FIRST, CX), :]
        pltpu.make_async_copy(whole, whole, rhs_sem.at[g]).wait()

        @pl.loop(0, LZ * (CX // 8))
        def _(t):
            l, xt = t // 4, lax.rem(t, 4)
            at = pl.ds(xt * 8, 8)
            own = pl.ds(xt * 8 + FIRST, 8)
            back = 1.0 / scale[l, own, :]
            mat = [inv_v[n * LZ + l, at, :] * back for n in range(9)]

            @pl.when(g == 0)
            def _():
                for n in range(9):
                    mats[n * LZ + l, at, :] = mat[n] * back

            for j in range(GC):
                base = (g * GC + j) * 3 * LZ + l
                r = [q0[base + c * LZ, own, :] for c in range(3)]
                for c in range(3):
                    q0[base + c * LZ, own, :] = (
                        mat[3 * c] * r[0] + mat[3 * c + 1] * r[1] + mat[3 * c + 2] * r[2]
                    )

        halo_start(q0, 0, g)

    pl.when(has_right)(to_right.wait_send)
    pl.when(has_left)(to_right.wait_recv)
    pl.when(has_left)(to_left.wait_send)
    pl.when(has_right)(to_left.wait_recv)

    @pl.loop(0, LZ * (CX // 8))
    def _(t):
        l, xt = t // 4, lax.rem(t, 4)
        at = pl.ds(xt * 8, 8)
        own = pl.ds(xt * 8 + FIRST, 8)
        txm[l, at, :] = edge[l, own, :] * scale[l, pl.ds(xt * 8 + LOW, 8), :]
        txp[l, at, :] = scale[l, own, :] * edge[l, pl.ds(xt * 8 + FIRST + 1, 8), :]

    def tile(src, dst, g, l, xt, below, above):
        at = pl.ds(xt * 8, 8)
        own = pl.ds(xt * 8 + FIRST, 8)
        xlo = pl.ds(xt * 8 + LOW, 8)
        xhi = pl.ds(xt * 8 + FIRST + 1, 8)
        am, ap, bm, bp = (ref[l, at, :] for ref in (txm, txp, tym, typ))
        mat = [mats[n * LZ + l, at, :] for n in range(9)]
        for j in range(GC):
            base = (g * GC + j) * 3 * LZ + l
            sums = []
            for c in range(3):
                b = base + c * LZ
                mid = src[b, own, :]
                s = am * src[b, xlo, :] + ap * src[b, xhi, :]
                s = s + (bm * pltpu.roll(mid, 1, axis=1) + bp * pltpu.roll(mid, NY - 1, axis=1))
                if below and above:
                    s = s + (src[b - 1, own, :] + src[b + 1, own, :])
                elif below:
                    s = s + src[b - 1, own, :]
                else:
                    s = s + src[b + 1, own, :]
                sums.append(s)
            for c in range(3):
                b = base + c * LZ
                dst[b, own, :] = (q0[b, own, :] + mat[3 * c] * sums[0]) + (
                    mat[3 * c + 1] * sums[1] + mat[3 * c + 2] * sums[2]
                )

    chain = [q0, qa, qb, qa, qb]
    for k in range(SWEEPS):
        src, dst = chain[k], chain[k + 1]

        @pl.loop(0, GROUPS)
        def _(g):
            halo_wait(src, k, g)

            @pl.loop(0, CX // 8)
            def _(xt):
                tile(src, dst, g, 0, xt, False, True)

                @pl.loop(1, LZ - 1)
                def _(l):
                    tile(src, dst, g, l, xt, True, True)

                tile(src, dst, g, LZ - 1, xt, True, False)

            if k < SWEEPS - 1:
                halo_start(dst, k + 1, g)

    panel = chain[SWEEPS]

    for copy in c_small:
        copy.wait()
    flat = panel.reshape(BLOCKS * ROWS, NY)
    lane16 = lax.broadcasted_iota(jnp.int32, (COLS, NY), 1)
    lane1 = lax.broadcasted_iota(jnp.int32, (1, NY), 1)
    live = count_s[0, 0]

    def slot(s, acc):
        at, w = cell_s[0, s], well_s[0, s]
        l, x, y = at // (CX * NY), lax.rem(at // NY, CX), lax.rem(at, NY)
        w = jnp.where(s < live, w, -1)
        line = None
        for c in range(3):
            part = coef_s[c, 0, s] * flat[
                pl.ds((c * LZ + l) * ROWS + FIRST + x, COLS, stride=3 * LZ * ROWS), :
            ]
            line = part if line is None else line + part
        mask = jnp.where(lane1 == y, scale[l, pl.ds(FIRST + x, 1), :], 0.0)
        line = pltpu.roll(line * mask, (w - y) & (NY - 1), axis=1)
        return tuple(
            acc[h] + jnp.where(lane16 == w - h * NY, line, 0.0) for h in range(2)
        )

    acc = lax.fori_loop(0, SLOTS, slot, (jnp.zeros((COLS, NY), f32),) * 2)
    for h in range(2):
        rows[h * COLS : (h + 1) * COLS, :] = acc[h]

    def rs_copy(i):
        there = lax.rem(dom + i, DOM)
        return remote(
            rows.at[pl.ds(there, 1)], parts.at[pl.ds(dom, 1)], rs_send.at[i], rs_recv.at[i],
            dom=there,
        )

    @pl.loop(1, DOM)
    def _(i):
        rs_copy(i).start()

    parts[pl.ds(dom, 1), :] = rows[pl.ds(dom, 1), :]

    @pl.loop(1, RES)
    def _(i):
        node_copy(i).wait()

    sub = lax.broadcasted_iota(jnp.int32, (256, WELLS), 0)
    for r in range(RES):
        ids = nodes[r : r + 1, :]
        hot[:, r * WELLS : (r + 1) * WELLS] = jnp.where((ids & 255) == sub, 1.0, 0.0).astype(
            jnp.bfloat16
        )

    @pl.loop(1, DOM)
    def _(i):
        rs_copy(i).wait()

    mine = res * 4 + zlo
    every[mine, pl.ds(yc, 1), :] = jnp.sum(parts[...], axis=0, keepdims=True)

    def ga_copy(i):
        r, d = peer_a(i)
        one = every.at[mine, pl.ds(yc, 1), :]
        return remote(one, one, ga_send.at[i], ga_recv.at[i], res=r, dom=d)

    @pl.loop(1, 32)
    def _(i):
        ga_copy(i).start()

    @pl.loop(1, 32)
    def _(i):
        ga_copy(i).wait()

    def gb_copy(i):
        some = every.at[:, yc, :]
        return remote(
            some, some, gb_send.at[i], gb_recv.at[i], dom=zlo * 8 + lax.rem(yc + i, 8)
        )

    @pl.loop(1, 8)
    def _(i):
        gb_copy(i).start()

    @pl.loop(1, 8)
    def _(i):
        gb_copy(i).wait()

    for r in range(RES):
        high = nodes[r : r + 1, :] // 256
        w = jnp.concatenate(
            [
                jnp.concatenate([every[4 * r], every[4 * r + 2]], axis=1),
                jnp.concatenate([every[4 * r + 1], every[4 * r + 3]], axis=1),
            ],
            axis=0,
        )
        for part in range(PIECES):
            now = w.astype(jnp.bfloat16).astype(f32)
            w = w - now
            for hi in range(8):
                at = (hi * PIECES + part) * COLS
                lhs[at : at + COLS, r * WELLS : (r + 1) * WELLS] = jnp.where(
                    high == hi, now, 0.0
                ).astype(jnp.bfloat16)
    spread = lax.dot_general(
        lhs[...], hot[...], (((1,), (1,)), ((), ())), preferred_element_type=f32
    )
    weight = jnp.zeros((COLS, 256), f32)
    for hi in range(8):
        total = None
        for part in range(PIECES):
            at = (hi * PIECES + part) * COLS
            now = spread[at : at + COLS]
            total = now if total is None else total + now
        at = slice(hi * 256, (hi + 1) * 256)
        schur = net_v[:, at] - total
        net_v[:, at] = schur
        weight = weight + schur * resid_v[:, at]
    c_schur = pltpu.make_async_copy(net_v, schur_out, out_sem.at[0])
    c_schur.start()
    wcol[...] = jnp.broadcast_to(
        jnp.sum(weight, axis=1, keepdims=True) * (1.0 / math.sqrt(NET)), (COLS, NY)
    )

    weights = [jnp.broadcast_to(wcol[j : j + 1, :], (8, NY)) for j in range(COLS)]

    @pl.loop(0, 3 * LZ)
    def _(b):
        l = lax.rem(b, LZ)
        for xt in range(CX // 8):
            own = pl.ds(xt * 8 + FIRST, 8)
            total = [None, None]
            for j in range(COLS):
                term = weights[j] * panel[j * 3 * LZ + b, own, :]
                total[j % 2] = term if total[j % 2] is None else total[j % 2] + term
            corr_v[b, xt * 8 : xt * 8 + 8, :] = scale[l, own, :] * (total[0] + total[1])

    c_corr = pltpu.make_async_copy(corr_v, corr_out, out_sem.at[1])
    c_corr.start()
    c_schur.wait()
    c_corr.wait()


def local(rhs, inv, trans, cell, well, coef, count, node, net, resid):
    f32 = jnp.float32
    any_space = pl.BlockSpec(memory_space=pl.ANY)
    vmem = lambda *shape: pltpu.VMEM(shape, f32)
    dma = lambda *shape: pltpu.SemaphoreType.DMA(shape)
    corr, schur = pl.pallas_call(
        kernel,
        out_shape=(
            jax.ShapeDtypeStruct((3 * LZ, CX, NY), f32),
            jax.ShapeDtypeStruct((COLS, NET), f32),
        ),
        in_specs=[any_space] * 10,
        out_specs=[any_space] * 2,
        scratch_shapes=[
            vmem(BLOCKS, ROWS, NY), vmem(BLOCKS, ROWS, NY), vmem(BLOCKS, ROWS, NY),
            vmem(9 * LZ, CX, NY), vmem(3 * LZ, CX, NY),
            vmem(LZ, ROWS, NY), vmem(LZ, ROWS, NY),
            vmem(LZ, CX, NY), vmem(LZ, CX, NY), vmem(LZ, CX, NY), vmem(LZ, CX, NY),
            vmem(9 * LZ, CX, NY),
            pltpu.SMEM((1, SLOTS), jnp.int32), pltpu.SMEM((1, SLOTS), jnp.int32),
            pltpu.SMEM((3, 1, SLOTS), f32), pltpu.SMEM((1, 1), jnp.int32),
            pltpu.VMEM((RES, WELLS), jnp.int32), vmem(COLS, NET), vmem(1, NET),
            vmem(32, NY), vmem(32, NY), vmem(32, 8, NY),
            pltpu.VMEM((256, NET), jnp.bfloat16),
            pltpu.VMEM((8 * PIECES * COLS, NET), jnp.bfloat16),
            vmem(COLS, NY), vmem(3 * LZ, CX, NY),
            dma(9), dma(GROUPS),
            dma(SWEEPS, GROUPS, 2), dma(SWEEPS, GROUPS, 2), dma(2), dma(2),
            dma(RES), dma(RES), dma(DOM), dma(DOM), dma(32), dma(32), dma(8), dma(8), dma(2),
        ],
        compiler_params=pltpu.CompilerParams(
            collective_id=0, has_side_effects=True, vmem_limit_bytes=56 * 1024 * 1024
        ),
        cost_estimate=pl.CostEstimate(
            flops=120_000_000, bytes_accessed=8_500_000, transcendentals=0
        ),
    )(
        rhs.reshape(BLOCKS, CX, NY), inv.reshape(9 * LZ, CX, NY), trans.reshape(3 * LZ, CX, NY),
        cell, well, coef.transpose(1, 0, 2), count, node, net, resid.reshape(1, NET),
    )
    return corr.reshape(1, 3, LZ, CX, NY), schur


def solution(mesh):
    return jax.shard_map(
        local,
        mesh=mesh,
        in_specs=(
            P("res", None, None, "dom", None),
            P("res", None, None, None, "dom", None),
            P("res", None, None, "dom", None),
            P("res", "dom"),
            P("res", "dom"),
            P("res", None, "dom"),
            P("res", "dom"),
            P("res", None),
            P(),
            P(),
        ),
        out_specs=(P("res", None, None, "dom", None), P()),
        check_vma=False,
    )
```

time: 205 us -> 121 us (0.59)
  the two profiles are of different devices: /device:TPU:32 before, /device:TPU:1 now
where the time goes in v1:
time: 121 us
  Pallas kernels  116 us (96%)
  local copies, waits for them, and re-layouts  3.33 us (3%)
  between operations  1.29 us (1%)
    pallas_call x1, Pallas kernels, local(): pl.pallas_call(kernel, out_shape=(jax.ShapeDtypeStruct((3 * LZ, CX, NY),...  116 us
    unnamed x2, local copies, waits for them, and re-layouts  3.33 us

profile of v1, /device:TPU:1, one launch (start us, length us, event | category | flops | bytes accessed | tf_op | source)
XLA Modules:
  0.0 120.7 jit_solution(2401986717519454777)
XLA Ops:
  1.3 116.1 %shard_map.113 = (f32[24,32,128]{2,1,0:T(8,128)}, f32[16,2048]{1,0:T(8,128)}) custom-call(f32[384,32,128]{2,1,0:T(8,128)} %bitcast.6, f32[72,32,128]{2,1,0:T(8,128)} %bitcast.7, f32[24,32,128]{2,1,0:T(8,128)} %bitcast.8, s32[1,256]{1,0:T(1,128)} %cell.1, s32[1,256]{1,0:T(1,128)} %well.1, f32[3,1,256]{2,1,0:T(1,128)} %bitcast.11, s32[1,1]{1,0:T(1,128)S(6)} %copy.14.count, ...), custom_call_target="tpu_custom_call" | custom-call | flops 120000000 | bytes 8500000 | tf_op jit(solution)/shard_map/pallas_call | solution.py:423
  117.4 1.8 %copy.15 = f32[1,3,8,32,128]{4,3,2,1,0:T(8,128)} copy(f32[1,3,8,32,128]{4,3,2,1,0:T(8,128)} %bitcast.9) | data formatting | bytes 786432
  119.1 1.6 %copy.16 = f32[16,2048]{1,0:T(8,128)} copy(f32[16,2048]{1,0:T(8,128)} %get-tuple-element.9) | data formatting | bytes 262144

commit v2 on v1

--- a/solution.py
+++ b/solution.py
@@ -19,16 +19,18 @@
 BLOCKS = COLS * 3 * LZ
 GB = BLOCKS // GROUPS
 PIECES = 3
+PITCH = 3 * COLS + 1
 
 
 def kernel(
     rhs, inv, trans, cell, well, coef, count, node, net, resid,
     corr_out, schur_out,
     q0, qa, qb, inv_v, trans_v, scale, edge, txm, txp, tym, typ, mats,
-    cell_s, well_s, coef_s, count_s, nodes, net_v, resid_v,
-    rows, parts, every, hot, lhs, wcol, corr_v,
+    cell_v, well_v, coef_s, count_s, slots_v, slots_s, nodes, net_v, resid_v,
+    lines, rows, parts, sums, every, hot, lhs, wcol, corr_v,
     in_sem, rhs_sem, halo_send, halo_recv, edge_send, edge_recv,
-    node_send, node_recv, rs_send, rs_recv, ga_send, ga_recv, gb_send, gb_recv, out_sem,
+    node_send, node_recv, rs_send, rs_recv, ga_send, ga_recv, gb_send, gb_recv,
+    out_sem,
 ):
     f32 = jnp.float32
     res, dom = lax.axis_index("res"), lax.axis_index("dom")
@@ -42,8 +44,8 @@
     c_inv = local(inv, inv_v, 1)
     c_node = local(node, nodes.at[pl.ds(res, 1)], 2)
     c_small = [
-        local(cell, cell_s, 3),
-        local(well, well_s, 4),
+        local(cell, cell_v, 3),
+        local(well, well_v, 4),
         local(coef, coef_s, 5),
         local(count, count_s, 6),
         local(net, net_v, 7),
@@ -67,25 +69,25 @@
 
     barrier = pltpu.get_barrier_semaphore()
 
-    @pl.loop(1, DOM)
-    def _(i):
-        pl.semaphore_signal(
-            barrier, inc=1, device_id={"dom": lax.rem(dom + i, DOM)}, device_id_type=MESH
-        )
-
-    def peer_a(i):
+    def greet(**where):
+        pl.semaphore_signal(barrier, inc=1, device_id=where, device_id_type=MESH)
+
+    def plane(i):
+        return zlo * 8 + lax.rem(yc + i, 8)
+
+    def column(i):
         there = lax.rem(res * 4 + zlo + i, 32)
         return there // 4, lax.rem(there, 4) * 8 + yc
 
-    @pl.loop(1, RES)
-    def _(i):
-        for z in range(4):
-            pl.semaphore_signal(
-                barrier,
-                inc=1,
-                device_id={"res": lax.rem(res + i, RES), "dom": z * 8 + yc},
-                device_id_type=MESH,
-            )
+    greet(dom=lax.rem(dom + 1, DOM))
+    greet(dom=lax.rem(dom + DOM - 1, DOM))
+    for i in range(1, 8):
+        greet(dom=plane(i))
+
+    @pl.loop(1, 32)
+    def _(i):
+        r, d = column(i)
+        greet(res=r, dom=d)
 
     lane = lax.broadcasted_iota(jnp.int32, (8, NY), 1)
 
@@ -105,26 +107,8 @@
             tym[l, at, :] = jnp.where(lane == 0, 0.0, ty * e * pltpu.roll(e, 1, axis=1))
             typ[l, at, :] = jnp.where(lane == NY - 1, 0.0, e * pltpu.roll(ty * e, NY - 1, axis=1))
 
-    @pl.when(jnp.logical_not(has_left))
-    def _():
-        scale[:, LOW : LOW + 1, :] = jnp.zeros((LZ, 1, NY), f32)
-        for buf in (q0, qa, qb):
-
-            @pl.loop(0, BLOCKS)
-            def _(b):
-                buf[b, LOW : LOW + 1, :] = jnp.zeros((1, NY), f32)
-
-    @pl.when(jnp.logical_not(has_right))
-    def _():
-        edge[:, HIGH : HIGH + 1, :] = jnp.zeros((LZ, 1, NY), f32)
-        for buf in (q0, qa, qb):
-
-            @pl.loop(0, BLOCKS)
-            def _(b):
-                buf[b, HIGH : HIGH + 1, :] = jnp.zeros((1, NY), f32)
-
     c_node.wait()
-    pl.semaphore_wait(barrier, DOM - 1 + 4 * (RES - 1))
+    pl.semaphore_wait(barrier, 2 + 7 + 31)
 
     def remote(src, dst, send, recv, **where):
         return pltpu.make_async_remote_copy(
@@ -180,33 +164,62 @@
             halo(buf, k, g, 1).wait_send()
             halo(buf, k, g, 0).wait_recv()
 
+    for copy in c_small:
+        copy.wait()
+    at, to = cell_v[...], well_v[...]
+    number = lax.broadcasted_iota(jnp.int32, (1, SLOTS), 1)
+    slots_v[0:1, :] = (at // NY) * PITCH
+    slots_v[1:2, :] = (to - at) & (NY - 1)
+    slots_v[2:3, :] = jnp.where(number < count_s[0, 0], to, -1)
+    c_slots = local(slots_v, slots_s, 9)
+    c_slots.start()
+
+    def clear(row, faces):
+        faces[:, row : row + 1, :] = jnp.zeros((LZ, 1, NY), f32)
+
+        @pl.loop(0, BLOCKS // 8)
+        def _(b):
+            for i in range(8):
+                for buf in (q0, qa, qb):
+                    buf[b * 8 + i, row : row + 1, :] = jnp.zeros((1, NY), f32)
+
+    @pl.when(jnp.logical_not(has_left))
+    def _():
+        clear(LOW, scale)
+
+    @pl.when(jnp.logical_not(has_right))
+    def _():
+        clear(HIGH, edge)
+
     c_inv.wait()
+
+    @pl.loop(0, LZ * (CX // 8))
+    def _(t):
+        l, xt = t // 4, lax.rem(t, 4)
+        at = pl.ds(xt * 8, 8)
+        back = 1.0 / scale[l, pl.ds(xt * 8 + FIRST, 8), :]
+        for n in range(9):
+            mat = inv_v[n * LZ + l, at, :] * back
+            inv_v[n * LZ + l, at, :] = mat
+            mats[n * LZ + l, at, :] = mat * back
 
     @pl.loop(0, GROUPS)
     def _(g):
         whole = q0.at[pl.ds(g * GB, GB), pl.ds(FIRST, CX), :]
         pltpu.make_async_copy(whole, whole, rhs_sem.at[g]).wait()
 
-        @pl.loop(0, LZ * (CX // 8))
-        def _(t):
-            l, xt = t // 4, lax.rem(t, 4)
-            at = pl.ds(xt * 8, 8)
-            own = pl.ds(xt * 8 + FIRST, 8)
-            back = 1.0 / scale[l, own, :]
-            mat = [inv_v[n * LZ + l, at, :] * back for n in range(9)]
-
-            @pl.when(g == 0)
-            def _():
-                for n in range(9):
-                    mats[n * LZ + l, at, :] = mat[n] * back
-
-            for j in range(GC):
-                base = (g * GC + j) * 3 * LZ + l
-                r = [q0[base + c * LZ, own, :] for c in range(3)]
-                for c in range(3):
-                    q0[base + c * LZ, own, :] = (
-                        mat[3 * c] * r[0] + mat[3 * c + 1] * r[1] + mat[3 * c + 2] * r[2]
-                    )
+        @pl.loop(0, LZ)
+        def _(l):
+            for xt in range(CX // 8):
+                own = slice(xt * 8 + FIRST, xt * 8 + FIRST + 8)
+                mat = [inv_v[n * LZ + l, xt * 8 : xt * 8 + 8, :] for n in range(9)]
+                for j in range(GC):
+                    base = (g * GC + j) * 3 * LZ + l
+                    r = [q0[base + c * LZ, own, :] for c in range(3)]
+                    for c in range(3):
+                        q0[base + c * LZ, own, :] = (
+                            mat[3 * c] * r[0] + mat[3 * c + 1] * r[1] + mat[3 * c + 2] * r[2]
+                        )
 
         halo_start(q0, 0, g)
 
@@ -223,11 +236,11 @@
         txm[l, at, :] = edge[l, own, :] * scale[l, pl.ds(xt * 8 + LOW, 8), :]
         txp[l, at, :] = scale[l, own, :] * edge[l, pl.ds(xt * 8 + FIRST + 1, 8), :]
 
-    def tile(src, dst, g, l, xt, below, above):
-        at = pl.ds(xt * 8, 8)
-        own = pl.ds(xt * 8 + FIRST, 8)
-        xlo = pl.ds(xt * 8 + LOW, 8)
-        xhi = pl.ds(xt * 8 + FIRST + 1, 8)
+    def tile(src, dst, g, l, xt, below, above, last):
+        at = slice(xt * 8, xt * 8 + 8)
+        own = slice(xt * 8 + FIRST, xt * 8 + FIRST + 8)
+        xlo = slice(xt * 8 + LOW, xt * 8 + LOW + 8)
+        xhi = slice(xt * 8 + FIRST + 1, xt * 8 + FIRST + 9)
         am, ap, bm, bp = (ref[l, at, :] for ref in (txm, txp, tym, typ))
         mat = [mats[n * LZ + l, at, :] for n in range(9)]
         for j in range(GC):
@@ -247,72 +260,64 @@
                 sums.append(s)
             for c in range(3):
                 b = base + c * LZ
-                dst[b, own, :] = (q0[b, own, :] + mat[3 * c] * sums[0]) + (
+                out = (q0[b, own, :] + mat[3 * c] * sums[0]) + (
                     mat[3 * c + 1] * sums[1] + mat[3 * c + 2] * sums[2]
                 )
+                if last:
+                    out = out * scale[l, own, :]
+                    line = (l * CX + xt * 8) * PITCH + c * COLS + g * GC + j
+                    lines[pl.ds(line, 8, stride=PITCH), :] = out
+                dst[b, own, :] = out
 
     chain = [q0, qa, qb, qa, qb]
     for k in range(SWEEPS):
-        src, dst = chain[k], chain[k + 1]
+        src, dst, last = chain[k], chain[k + 1], k == SWEEPS - 1
+
+        def part(g, columns, src=src, dst=dst, last=last):
+            for l in range(LZ):
+                for xt in columns:
+                    tile(src, dst, g, l, xt, l > 0, l < LZ - 1, last)
 
         @pl.loop(0, GROUPS)
         def _(g):
             halo_wait(src, k, g)
-
-            @pl.loop(0, CX // 8)
-            def _(xt):
-                tile(src, dst, g, 0, xt, False, True)
-
-                @pl.loop(1, LZ - 1)
-                def _(l):
-                    tile(src, dst, g, l, xt, True, True)
-
-                tile(src, dst, g, LZ - 1, xt, True, False)
-
-            if k < SWEEPS - 1:
+            part(g, (0, CX // 8 - 1))
+            if not last:
                 halo_start(dst, k + 1, g)
+            part(g, range(1, CX // 8 - 1))
 
     panel = chain[SWEEPS]
 
-    for copy in c_small:
-        copy.wait()
-    flat = panel.reshape(BLOCKS * ROWS, NY)
-    lane16 = lax.broadcasted_iota(jnp.int32, (COLS, NY), 1)
-    lane1 = lax.broadcasted_iota(jnp.int32, (1, NY), 1)
-    live = count_s[0, 0]
+    c_slots.wait()
+    lane = lax.broadcasted_iota(jnp.int32, (COLS, NY), 1)
 
     def slot(s, acc):
-        at, w = cell_s[0, s], well_s[0, s]
-        l, x, y = at // (CX * NY), lax.rem(at // NY, CX), lax.rem(at, NY)
-        w = jnp.where(s < live, w, -1)
+        base, turn, w = (slots_s[i, s] for i in range(3))
         line = None
         for c in range(3):
-            part = coef_s[c, 0, s] * flat[
-                pl.ds((c * LZ + l) * ROWS + FIRST + x, COLS, stride=3 * LZ * ROWS), :
-            ]
+            part = coef_s[c, 0, s] * lines[pl.ds(base + c * COLS, COLS), :]
             line = part if line is None else line + part
-        mask = jnp.where(lane1 == y, scale[l, pl.ds(FIRST + x, 1), :], 0.0)
-        line = pltpu.roll(line * mask, (w - y) & (NY - 1), axis=1)
-        return tuple(
-            acc[h] + jnp.where(lane16 == w - h * NY, line, 0.0) for h in range(2)
-        )
-
-    acc = lax.fori_loop(0, SLOTS, slot, (jnp.zeros((COLS, NY), f32),) * 2)
+        line = pltpu.roll(line, turn, axis=1)
+        return tuple(acc[h] + jnp.where(lane == w - h * NY, line, 0.0) for h in range(2))
+
+    acc = lax.fori_loop(0, SLOTS, slot, (jnp.zeros((COLS, NY), f32),) * 2, unroll=8)
     for h in range(2):
-        rows[h * COLS : (h + 1) * COLS, :] = acc[h]
+        for half in range(2):
+            rows[2 * h + half] = acc[h][half * 8 : half * 8 + 8]
 
     def rs_copy(i):
-        there = lax.rem(dom + i, DOM)
+        there = plane(i)
         return remote(
-            rows.at[pl.ds(there, 1)], parts.at[pl.ds(dom, 1)], rs_send.at[i], rs_recv.at[i],
-            dom=there,
-        )
-
-    @pl.loop(1, DOM)
+            rows.at[:, lax.rem(there, 8), :], parts.at[yc, pl.ds(0, 4), :], rs_send.at[i],
+            rs_recv.at[i], dom=there,
+        )
+
+    @pl.loop(1, 8)
     def _(i):
         rs_copy(i).start()
 
-    parts[pl.ds(dom, 1), :] = rows[pl.ds(dom, 1), :]
+    for z in range(4):
+        parts[yc, z : z + 1, :] = rows[z, pl.ds(yc, 1), :]
 
     @pl.loop(1, RES)
     def _(i):
@@ -325,17 +330,20 @@
             jnp.bfloat16
         )
 
-    @pl.loop(1, DOM)
+    @pl.loop(1, 8)
     def _(i):
         rs_copy(i).wait()
 
+    total = parts[0, 0:4, :]
+    for i in range(1, 8):
+        total = total + parts[i, 0:4, :]
     mine = res * 4 + zlo
-    every[mine, pl.ds(yc, 1), :] = jnp.sum(parts[...], axis=0, keepdims=True)
+    sums[mine, 0:4, :] = total
 
     def ga_copy(i):
-        r, d = peer_a(i)
-        one = every.at[mine, pl.ds(yc, 1), :]
-        return remote(one, one, ga_send.at[i], ga_recv.at[i], res=r, dom=d)
+        r, d = column(i)
+        some = sums.at[mine, pl.ds(0, 4), :]
+        return remote(some, some, ga_send.at[i], ga_recv.at[i], res=r, dom=d)
 
     @pl.loop(1, 32)
     def _(i):
@@ -344,11 +352,18 @@
     @pl.loop(1, 32)
     def _(i):
         ga_copy(i).wait()
+
+    for r in range(RES):
+        total = (sums[4 * r, 0:4, :] + sums[4 * r + 1, 0:4, :]) + (
+            sums[4 * r + 2, 0:4, :] + sums[4 * r + 3, 0:4, :]
+        )
+        for z in range(4):
+            every[4 * r + z, pl.ds(yc, 1), :] = total[z : z + 1]
 
     def gb_copy(i):
         some = every.at[:, yc, :]
         return remote(
-            some, some, gb_send.at[i], gb_recv.at[i], dom=zlo * 8 + lax.rem(yc + i, 8)
+            some, some, gb_send.at[i], gb_recv.at[i], dom=plane(i)
         )
 
     @pl.loop(1, 8)
@@ -400,19 +415,34 @@
 
     @pl.loop(0, 3 * LZ)
     def _(b):
-        l = lax.rem(b, LZ)
         for xt in range(CX // 8):
-            own = pl.ds(xt * 8 + FIRST, 8)
+            own = slice(xt * 8 + FIRST, xt * 8 + FIRST + 8)
             total = [None, None]
             for j in range(COLS):
                 term = weights[j] * panel[j * 3 * LZ + b, own, :]
                 total[j % 2] = term if total[j % 2] is None else total[j % 2] + term
-            corr_v[b, xt * 8 : xt * 8 + 8, :] = scale[l, own, :] * (total[0] + total[1])
+            corr_v[b, xt * 8 : xt * 8 + 8, :] = total[0] + total[1]
 
     c_corr = pltpu.make_async_copy(corr_v, corr_out, out_sem.at[1])
     c_corr.start()
     c_schur.wait()
     c_corr.wait()
+
+
+def hand_over(corr, schur, corr_out, schur_out, corr_v, schur_v, sem_in, sem_out):
+    pieces = [(schur, schur_v, schur_out)]
+    for i in range(3):
+        at = pl.ds(i * LZ, LZ)
+        pieces.append((corr.at[at], corr_v.at[at], corr_out.at[at]))
+    into = [pltpu.make_async_copy(p[0], p[1], sem_in.at[i]) for i, p in enumerate(pieces)]
+    away = [pltpu.make_async_copy(p[1], p[2], sem_out.at[i]) for i, p in enumerate(pieces)]
+    for copy in into:
+        copy.start()
+    for first, then in zip(into, away):
+        first.wait()
+        then.start()
+    for copy in away:
+        copy.wait()
 
 
 def local(rhs, inv, trans, cell, well, coef, count, node, net, resid):
@@ -434,16 +464,18 @@
             vmem(LZ, ROWS, NY), vmem(LZ, ROWS, NY),
             vmem(LZ, CX, NY), vmem(LZ, CX, NY), vmem(LZ, CX, NY), vmem(LZ, CX, NY),
             vmem(9 * LZ, CX, NY),
-            pltpu.SMEM((1, SLOTS), jnp.int32), pltpu.SMEM((1, SLOTS), jnp.int32),
+            pltpu.VMEM((1, SLOTS), jnp.int32), pltpu.VMEM((1, SLOTS), jnp.int32),
             pltpu.SMEM((3, 1, SLOTS), f32), pltpu.SMEM((1, 1), jnp.int32),
+            pltpu.VMEM((8, SLOTS), jnp.int32), pltpu.SMEM((8, SLOTS), jnp.int32),
             pltpu.VMEM((RES, WELLS), jnp.int32), vmem(COLS, NET), vmem(1, NET),
-            vmem(32, NY), vmem(32, NY), vmem(32, 8, NY),
+            vmem(LZ * CX * PITCH, NY),
+            vmem(4, 8, NY), vmem(8, 8, NY), vmem(32, 8, NY), vmem(32, 8, NY),
             pltpu.VMEM((256, NET), jnp.bfloat16),
             pltpu.VMEM((8 * PIECES * COLS, NET), jnp.bfloat16),
             vmem(COLS, NY), vmem(3 * LZ, CX, NY),
-            dma(9), dma(GROUPS),
+            dma(10), dma(GROUPS),
             dma(SWEEPS, GROUPS, 2), dma(SWEEPS, GROUPS, 2), dma(2), dma(2),
-            dma(RES), dma(RES), dma(DOM), dma(DOM), dma(32), dma(32), dma(8), dma(8), dma(2),
+            dma(RES), dma(RES), dma(8), dma(8), dma(32), dma(32), dma(8), dma(8), dma(2),
         ],
         compiler_params=pltpu.CompilerParams(
             collective_id=0, has_side_effects=True, vmem_limit_bytes=56 * 1024 * 1024
@@ -455,6 +487,16 @@
         rhs.reshape(BLOCKS, CX, NY), inv.reshape(9 * LZ, CX, NY), trans.reshape(3 * LZ, CX, NY),
         cell, well, coef.transpose(1, 0, 2), count, node, net, resid.reshape(1, NET),
     )
+    corr, schur = pl.pallas_call(
+        hand_over,
+        out_shape=(
+            jax.ShapeDtypeStruct((3 * LZ, CX, NY), f32),
+            jax.ShapeDtypeStruct((COLS, NET), f32),
+        ),
+        in_specs=[any_space] * 2,
+        out_specs=[any_space] * 2,
+        scratch_shapes=[vmem(3 * LZ, CX, NY), vmem(COLS, NET), dma(4), dma(4)],
+    )(corr, schur)
     return corr.reshape(1, 3, LZ, CX, NY), schur
 
 

time: 121 us -> 55.9 us (0.46)
  Pallas kernels: 116 us -> 54.5 us
  local copies, waits for them, and re-layouts: 3.33 us -> 0 us
    pallas_call x1, Pallas kernels: 116 us -> 52.7 us  [local(): pl.pallas_call(kernel, out_shape=(jax.ShapeDtypeStruct((3 * LZ, CX, NY),...]
    unnamed x2 -> x0, local copies, waits for them, and re-layouts: 3.33 us -> none
    pallas_call x0 -> x1, Pallas kernels: none -> 1.82 us  [local(): pl.pallas_call(hand_over, out_shape=(jax.ShapeDtypeStruct((3 * LZ, CX, NY...]
where the time goes in v2:
time: 55.9 us; the launch traced here: 55.8 us
  Pallas kernels  54.5 us (97%)
  between operations  1.29 us (2%)
    pallas_call x1, Pallas kernels, local(): pl.pallas_call(kernel, out_shape=(jax.ShapeDtypeStruct((3 * LZ, CX, NY),...  52.7 us
    pallas_call x1, Pallas kernels, local(): pl.pallas_call(hand_over, out_shape=(jax.ShapeDtypeStruct((3 * LZ, CX, NY...  1.82 us

profile of v2, /device:TPU:1, one launch (start us, length us, event | category | flops | bytes accessed | tf_op | source)
XLA Modules:
  0.0 55.8 jit_solution(14613631836099007958)
XLA Ops:
  1.3 52.7 %shard_map.113 = (f32[24,32,128]{2,1,0:T(8,128)}, f32[16,2048]{1,0:T(8,128)}) custom-call(f32[384,32,128]{2,1,0:T(8,128)} %bitcast.6, f32[72,32,128]{2,1,0:T(8,128)} %bitcast.7, f32[24,32,128]{2,1,0:T(8,128)} %bitcast.8, s32[1,256]{1,0:T(1,128)} %cell.1, s32[1,256]{1,0:T(1,128)} %well.1, f32[3,1,256]{2,1,0:T(1,128)} %bitcast.10, s32[1,1]{1,0:T(1,128)S(6)} %copy.12.count, ...), custom_call_target="tpu_custom_call" | custom-call | flops 120000000 | bytes 8500000 | tf_op jit(solution)/shard_map/pallas_call | solution.py:453
  53.9 1.8 %shard_map.114 = (f32[24,32,128]{2,1,0:T(8,128)}, f32[16,2048]{1,0:T(8,128)}) custom-call(f32[24,32,128]{2,1,0:T(8,128)} %get-tuple-element.6.corr, f32[16,2048]{1,0:T(8,128)} %get-tuple-element.7.schur), custom_call_target="tpu_custom_call" | custom-call | tf_op jit(solution)/shard_map/pallas_call | solution.py:490

commit v3 on v2

--- a/solution.py
+++ b/solution.py
@@ -27,10 +27,10 @@
     corr_out, schur_out,
     q0, qa, qb, inv_v, trans_v, scale, edge, txm, txp, tym, typ, mats,
     cell_v, well_v, coef_s, count_s, slots_v, slots_s, nodes, net_v, resid_v,
-    lines, rows, parts, sums, every, hot, lhs, wcol, corr_v,
+    lines, rows, parts, sums, hot, lhs, wcol, schur_v,
     in_sem, rhs_sem, halo_send, halo_recv, edge_send, edge_recv,
-    node_send, node_recv, rs_send, rs_recv, ga_send, ga_recv, gb_send, gb_recv,
-    out_sem,
+    node_send, node_recv, rs_send, rs_recv, ga_send, ga_recv, gw_send, gw_recv, gb_send,
+    gb_recv,
 ):
     f32 = jnp.float32
     res, dom = lax.axis_index("res"), lax.axis_index("dom")
@@ -48,8 +48,6 @@
         local(well, well_v, 4),
         local(coef, coef_s, 5),
         local(count, count_s, 6),
-        local(net, net_v, 7),
-        local(resid, resid_v, 8),
     ]
     c_trans.start()
     c_node.start()
@@ -66,6 +64,13 @@
 
     for copy in c_small:
         copy.start()
+    for hi in range(8):
+        at = pl.ds(hi * 256, 256)
+        for half in range(2):
+            local(
+                net.at[pl.ds(half * 8 + yc, 1), at], net_v.at[half, pl.ds(hi, 1), :], 7
+            ).start()
+        local(resid.at[:, at], resid_v.at[pl.ds(hi, 1), :], 8).start()
 
     barrier = pltpu.get_barrier_semaphore()
 
@@ -129,7 +134,7 @@
 
     def node_copy(i):
         return remote(
-            nodes.at[pl.ds(res, 1)], nodes.at[pl.ds(res, 1)], node_send.at[i], node_recv.at[i],
+            nodes.at[pl.ds(res, 1)], nodes.at[pl.ds(res, 1)], node_send, node_recv,
             res=lax.rem(res + i, RES),
         )
 
@@ -300,7 +305,7 @@
         line = pltpu.roll(line, turn, axis=1)
         return tuple(acc[h] + jnp.where(lane == w - h * NY, line, 0.0) for h in range(2))
 
-    acc = lax.fori_loop(0, SLOTS, slot, (jnp.zeros((COLS, NY), f32),) * 2, unroll=8)
+    acc = lax.fori_loop(0, SLOTS, slot, (jnp.zeros((COLS, NY), f32),) * 2, unroll=16)
     for h in range(2):
         for half in range(2):
             rows[2 * h + half] = acc[h][half * 8 : half * 8 + 8]
@@ -308,8 +313,8 @@
     def rs_copy(i):
         there = plane(i)
         return remote(
-            rows.at[:, lax.rem(there, 8), :], parts.at[yc, pl.ds(0, 4), :], rs_send.at[i],
-            rs_recv.at[i], dom=there,
+            rows.at[:, lax.rem(there, 8), :], parts.at[yc, pl.ds(0, 4), :], rs_send, rs_recv,
+            dom=there,
         )
 
     @pl.loop(1, 8)
@@ -319,9 +324,11 @@
     for z in range(4):
         parts[yc, z : z + 1, :] = rows[z, pl.ds(yc, 1), :]
 
-    @pl.loop(1, RES)
-    def _(i):
-        node_copy(i).wait()
+    def wait_all(ref, *sems):
+        for sem in sems:
+            pltpu.make_async_copy(ref, ref, sem).wait()
+
+    wait_all(nodes.at[pl.ds(0, RES - 1)], node_send, node_recv)
 
     sub = lax.broadcasted_iota(jnp.int32, (256, WELLS), 0)
     for r in range(RES):
@@ -330,9 +337,7 @@
             jnp.bfloat16
         )
 
-    @pl.loop(1, 8)
-    def _(i):
-        rs_copy(i).wait()
+    wait_all(parts.at[pl.ds(0, 7), pl.ds(0, 4), :], rs_send, rs_recv)
 
     total = parts[0, 0:4, :]
     for i in range(1, 8):
@@ -343,75 +348,64 @@
     def ga_copy(i):
         r, d = column(i)
         some = sums.at[mine, pl.ds(0, 4), :]
-        return remote(some, some, ga_send.at[i], ga_recv.at[i], res=r, dom=d)
+        return remote(some, some, ga_send, ga_recv, res=r, dom=d)
 
     @pl.loop(1, 32)
     def _(i):
         ga_copy(i).start()
 
-    @pl.loop(1, 32)
-    def _(i):
-        ga_copy(i).wait()
-
+    wait_all(net_v, in_sem.at[7])
+    wait_all(resid_v, in_sem.at[8])
+    wait_all(sums.at[pl.ds(0, 31), pl.ds(0, 4), :], ga_send, ga_recv)
+
+    sub8 = lax.broadcasted_iota(jnp.int32, (8, WELLS), 0)
     for r in range(RES):
-        total = (sums[4 * r, 0:4, :] + sums[4 * r + 1, 0:4, :]) + (
+        w = (sums[4 * r, 0:4, :] + sums[4 * r + 1, 0:4, :]) + (
             sums[4 * r + 2, 0:4, :] + sums[4 * r + 3, 0:4, :]
         )
-        for z in range(4):
-            every[4 * r + z, pl.ds(yc, 1), :] = total[z : z + 1]
-
-    def gb_copy(i):
-        some = every.at[:, yc, :]
-        return remote(
-            some, some, gb_send.at[i], gb_recv.at[i], dom=plane(i)
-        )
-
-    @pl.loop(1, 8)
-    def _(i):
-        gb_copy(i).start()
-
-    @pl.loop(1, 8)
-    def _(i):
-        gb_copy(i).wait()
-
-    for r in range(RES):
-        high = nodes[r : r + 1, :] // 256
-        w = jnp.concatenate(
-            [
-                jnp.concatenate([every[4 * r], every[4 * r + 2]], axis=1),
-                jnp.concatenate([every[4 * r + 1], every[4 * r + 3]], axis=1),
-            ],
-            axis=0,
-        )
+        here = nodes[r : r + 1, :] // 256 == sub8
         for part in range(PIECES):
             now = w.astype(jnp.bfloat16).astype(f32)
             w = w - now
-            for hi in range(8):
-                at = (hi * PIECES + part) * COLS
-                lhs[at : at + COLS, r * WELLS : (r + 1) * WELLS] = jnp.where(
-                    high == hi, now, 0.0
-                ).astype(jnp.bfloat16)
+            tiles = []
+            for half in range(2):
+                line = jnp.concatenate([now[half : half + 1], now[half + 2 : half + 3]], axis=1)
+                tiles.append(jnp.where(here, line, 0.0))
+            lhs[part * 16 : part * 16 + 16, r * WELLS : (r + 1) * WELLS] = jnp.concatenate(
+                tiles, axis=0
+            ).astype(jnp.bfloat16)
     spread = lax.dot_general(
         lhs[...], hot[...], (((1,), (1,)), ((), ())), preferred_element_type=f32
     )
-    weight = jnp.zeros((COLS, 256), f32)
-    for hi in range(8):
-        total = None
-        for part in range(PIECES):
-            at = (hi * PIECES + part) * COLS
-            now = spread[at : at + COLS]
-            total = now if total is None else total + now
-        at = slice(hi * 256, (hi + 1) * 256)
-        schur = net_v[:, at] - total
-        net_v[:, at] = schur
-        weight = weight + schur * resid_v[:, at]
-    c_schur = pltpu.make_async_copy(net_v, schur_out, out_sem.at[0])
-    c_schur.start()
-    wcol[...] = jnp.broadcast_to(
-        jnp.sum(weight, axis=1, keepdims=True) * (1.0 / math.sqrt(NET)), (COLS, NY)
-    )
-
-    weights = [jnp.broadcast_to(wcol[j : j + 1, :], (8, NY)) for j in range(COLS)]
+    spread = (spread[0:16] + spread[16:32]) + spread[32:48]
+    for half in range(2):
+        schur = net_v[half] - spread[half * 8 : half * 8 + 8]
+        schur_v[half, yc] = schur
+        weight = jnp.sum(schur * resid_v[...], axis=0, keepdims=True)
+        weight = jnp.sum(weight, axis=1, keepdims=True) * (1.0 / math.sqrt(NET))
+        wcol[half, pl.ds(yc, 1), :] = jnp.broadcast_to(weight, (1, NY))
+
+    def gw_copy(i):
+        some = wcol.at[:, yc, :]
+        return remote(some, some, gw_send, gw_recv, dom=plane(i))
+
+    def gb_copy(i):
+        some = schur_v.at[:, yc]
+        return remote(some, some, gb_send, gb_recv, dom=plane(i))
+
+    @pl.loop(1, 8)
+    def _(i):
+        gw_copy(i).start()
+
+    @pl.loop(1, 8)
+    def _(i):
+        gb_copy(i).start()
+
+    wait_all(wcol.at[:, pl.ds(0, 7), :], gw_send, gw_recv)
+
+    weights = [
+        jnp.broadcast_to(wcol[j // 8, j % 8 : j % 8 + 1, :], (8, NY)) for j in range(COLS)
+    ]
 
     @pl.loop(0, 3 * LZ)
     def _(b):
@@ -421,43 +415,29 @@
             for j in range(COLS):
                 term = weights[j] * panel[j * 3 * LZ + b, own, :]
                 total[j % 2] = term if total[j % 2] is None else total[j % 2] + term
-            corr_v[b, xt * 8 : xt * 8 + 8, :] = total[0] + total[1]
-
-    c_corr = pltpu.make_async_copy(corr_v, corr_out, out_sem.at[1])
-    c_corr.start()
-    c_schur.wait()
-    c_corr.wait()
-
-
-def hand_over(corr, schur, corr_out, schur_out, corr_v, schur_v, sem_in, sem_out):
-    pieces = [(schur, schur_v, schur_out)]
-    for i in range(3):
-        at = pl.ds(i * LZ, LZ)
-        pieces.append((corr.at[at], corr_v.at[at], corr_out.at[at]))
-    into = [pltpu.make_async_copy(p[0], p[1], sem_in.at[i]) for i, p in enumerate(pieces)]
-    away = [pltpu.make_async_copy(p[1], p[2], sem_out.at[i]) for i, p in enumerate(pieces)]
-    for copy in into:
-        copy.start()
-    for first, then in zip(into, away):
-        first.wait()
-        then.start()
-    for copy in away:
-        copy.wait()
+            corr_out[b, xt * 8 : xt * 8 + 8, :] = total[0] + total[1]
+
+    wait_all(schur_v.at[:, pl.ds(0, 7)], gb_send, gb_recv)
+    for half in range(2):
+        for place in range(8):
+            row = half * 8 + place
+            for hi in range(8):
+                schur_out[row : row + 1, hi * 256 : (hi + 1) * 256] = schur_v[
+                    half, place, hi : hi + 1, :
+                ]
 
 
 def local(rhs, inv, trans, cell, well, coef, count, node, net, resid):
     f32 = jnp.float32
     any_space = pl.BlockSpec(memory_space=pl.ANY)
+    vmem_space = pl.BlockSpec(memory_space=pltpu.VMEM)
     vmem = lambda *shape: pltpu.VMEM(shape, f32)
     dma = lambda *shape: pltpu.SemaphoreType.DMA(shape)
     corr, schur = pl.pallas_call(
         kernel,
-        out_shape=(
-            jax.ShapeDtypeStruct((3 * LZ, CX, NY), f32),
-            jax.ShapeDtypeStruct((COLS, NET), f32),
-        ),
+        out_shape=(vmem(3 * LZ, CX, NY), vmem(COLS, NET)),
         in_specs=[any_space] * 10,
-        out_specs=[any_space] * 2,
+        out_specs=[vmem_space] * 2,
         scratch_shapes=[
             vmem(BLOCKS, ROWS, NY), vmem(BLOCKS, ROWS, NY), vmem(BLOCKS, ROWS, NY),
             vmem(9 * LZ, CX, NY), vmem(3 * LZ, CX, NY),
@@ -467,15 +447,15 @@
             pltpu.VMEM((1, SLOTS), jnp.int32), pltpu.VMEM((1, SLOTS), jnp.int32),
             pltpu.SMEM((3, 1, SLOTS), f32), pltpu.SMEM((1, 1), jnp.int32),
             pltpu.VMEM((8, SLOTS), jnp.int32), pltpu.SMEM((8, SLOTS), jnp.int32),
-            pltpu.VMEM((RES, WELLS), jnp.int32), vmem(COLS, NET), vmem(1, NET),
+            pltpu.VMEM((RES, WELLS), jnp.int32), vmem(2, 8, 256), vmem(8, 256),
             vmem(LZ * CX * PITCH, NY),
-            vmem(4, 8, NY), vmem(8, 8, NY), vmem(32, 8, NY), vmem(32, 8, NY),
+            vmem(4, 8, NY), vmem(8, 8, NY), vmem(32, 8, NY),
             pltpu.VMEM((256, NET), jnp.bfloat16),
-            pltpu.VMEM((8 * PIECES * COLS, NET), jnp.bfloat16),
-            vmem(COLS, NY), vmem(3 * LZ, CX, NY),
+            pltpu.VMEM((16 * PIECES, NET), jnp.bfloat16),
+            vmem(2, 8, NY), vmem(2, 8, 8, 256),
             dma(10), dma(GROUPS),
             dma(SWEEPS, GROUPS, 2), dma(SWEEPS, GROUPS, 2), dma(2), dma(2),
-            dma(RES), dma(RES), dma(8), dma(8), dma(32), dma(32), dma(8), dma(8), dma(2),
+            *[pltpu.SemaphoreType.DMA] * 10,
         ],
         compiler_params=pltpu.CompilerParams(
             collective_id=0, has_side_effects=True, vmem_limit_bytes=56 * 1024 * 1024
@@ -487,16 +467,6 @@
         rhs.reshape(BLOCKS, CX, NY), inv.reshape(9 * LZ, CX, NY), trans.reshape(3 * LZ, CX, NY),
         cell, well, coef.transpose(1, 0, 2), count, node, net, resid.reshape(1, NET),
     )
-    corr, schur = pl.pallas_call(
-        hand_over,
-        out_shape=(
-            jax.ShapeDtypeStruct((3 * LZ, CX, NY), f32),
-            jax.ShapeDtypeStruct((COLS, NET), f32),
-        ),
-        in_specs=[any_space] * 2,
-        out_specs=[any_space] * 2,
-        scratch_shapes=[vmem(3 * LZ, CX, NY), vmem(COLS, NET), dma(4), dma(4)],
-    )(corr, schur)
     return corr.reshape(1, 3, LZ, CX, NY), schur
 
 

time: 55.9 us -> 51.8 us (0.927)
  Pallas kernels: 54.5 us -> 49 us
  local copies, waits for them, and re-layouts: 0 us -> 1.4 us
    pallas_call x2 -> x1, Pallas kernels: 54.5 us -> 49 us  [local(): pl.pallas_call(kernel, out_shape=(vmem(3 * LZ, CX, NY), vmem(COLS, NET)),...]
    unnamed x0 -> x2, local copies, waits for them, and re-layouts: none -> 1.4 us
where the time goes in v3:
time: 51.8 us; the launch traced here: 51.7 us
  Pallas kernels  49 us (95%)
  local copies, waits for them, and re-layouts  1.4 us (3%)
  between operations  1.29 us (2%)
    pallas_call x1, Pallas kernels, local(): pl.pallas_call(kernel, out_shape=(vmem(3 * LZ, CX, NY), vmem(COLS, NET)),...  49 us
    unnamed x2, local copies, waits for them, and re-layouts  1.4 us

profile of v3, /device:TPU:1, one launch (start us, length us, event | category | flops | bytes accessed | tf_op | source)
XLA Modules:
  0.0 51.7 jit_solution(8772739814327362276)
XLA Ops:
  1.3 49.0 %shard_map.113 = (f32[24,32,128]{2,1,0:T(8,128)S(1)}, f32[16,2048]{1,0:T(8,128)S(1)}) custom-call(f32[384,32,128]{2,1,0:T(8,128)} %bitcast.7, f32[72,32,128]{2,1,0:T(8,128)} %bitcast.8, f32[24,32,128]{2,1,0:T(8,128)} %bitcast.9, s32[1,256]{1,0:T(1,128)} %cell.1, s32[1,256]{1,0:T(1,128)} %well.1, f32[3,1,256]{2,1,0:T(1,128)} %bitcast.11, ...), custom_call_target="tpu_custom_call" | custom-call | flops 120000000 | bytes 8500000 | tf_op jit(solution)/shard_map/pallas_call | solution.py:436
  50.3 0.7 %copy.14 = f32[1,3,8,32,128]{4,3,2,1,0:T(8,128)} copy(f32[1,3,8,32,128]{4,3,2,1,0:T(8,128)S(1)} %bitcast.6) | data formatting | bytes 786432
  51.0 0.7 %copy.15 = f32[16,2048]{1,0:T(8,128)} copy(f32[16,2048]{1,0:T(8,128)S(1)} %get-tuple-element.7) | data formatting | bytes 262144

commit v4 on v3

--- a/solution.py
+++ b/solution.py
@@ -1,4 +1,3 @@
-import functools
 import math
 
 import jax
@@ -173,9 +172,12 @@
         copy.wait()
     at, to = cell_v[...], well_v[...]
     number = lax.broadcasted_iota(jnp.int32, (1, SLOTS), 1)
-    slots_v[0:1, :] = (at // NY) * PITCH
-    slots_v[1:2, :] = (to - at) & (NY - 1)
-    slots_v[2:3, :] = jnp.where(number < count_s[0, 0], to, -1)
+    numbers = (
+        (at // NY) * PITCH, (to - at) & (NY - 1), jnp.where(number < count_s[0, 0], to, -1)
+    )
+    for i, values in enumerate(numbers):
+        for half in range(2):
+            slots_v[half * 8 + i : half * 8 + i + 1, :] = values[:, half * 128 : half * 128 + 128]
     c_slots = local(slots_v, slots_s, 9)
     c_slots.start()
 
@@ -198,15 +200,15 @@
 
     c_inv.wait()
 
-    @pl.loop(0, LZ * (CX // 8))
-    def _(t):
-        l, xt = t // 4, lax.rem(t, 4)
-        at = pl.ds(xt * 8, 8)
-        back = 1.0 / scale[l, pl.ds(xt * 8 + FIRST, 8), :]
-        for n in range(9):
-            mat = inv_v[n * LZ + l, at, :] * back
-            inv_v[n * LZ + l, at, :] = mat
-            mats[n * LZ + l, at, :] = mat * back
+    @pl.loop(0, LZ)
+    def _(l):
+        for xt in range(CX // 8):
+            at = slice(xt * 8, xt * 8 + 8)
+            back = 1.0 / scale[l, xt * 8 + FIRST : xt * 8 + FIRST + 8, :]
+            for n in range(9):
+                mat = inv_v[n * LZ + l, at, :] * back
+                inv_v[n * LZ + l, at, :] = mat
+                mats[n * LZ + l, at, :] = mat * back
 
     @pl.loop(0, GROUPS)
     def _(g):
@@ -233,13 +235,10 @@
     pl.when(has_left)(to_left.wait_send)
     pl.when(has_right)(to_left.wait_recv)
 
-    @pl.loop(0, LZ * (CX // 8))
-    def _(t):
-        l, xt = t // 4, lax.rem(t, 4)
-        at = pl.ds(xt * 8, 8)
-        own = pl.ds(xt * 8 + FIRST, 8)
-        txm[l, at, :] = edge[l, own, :] * scale[l, pl.ds(xt * 8 + LOW, 8), :]
-        txp[l, at, :] = scale[l, own, :] * edge[l, pl.ds(xt * 8 + FIRST + 1, 8), :]
+    @pl.loop(0, LZ)
+    def _(l):
+        txm[l] = edge[l, FIRST : FIRST + CX, :] * scale[l, LOW : LOW + CX, :]
+        txp[l] = scale[l, FIRST : FIRST + CX, :] * edge[l, FIRST + 1 : FIRST + 1 + CX, :]
 
     def tile(src, dst, g, l, xt, below, above, last):
         at = slice(xt * 8, xt * 8 + 8)
@@ -296,16 +295,23 @@
     c_slots.wait()
     lane = lax.broadcasted_iota(jnp.int32, (COLS, NY), 1)
 
-    def slot(s, acc):
-        base, turn, w = (slots_s[i, s] for i in range(3))
+    def slot(half, s, acc):
+        base, turn, w = (slots_s[half * 8 + i, s] for i in range(3))
         line = None
         for c in range(3):
-            part = coef_s[c, 0, s] * lines[pl.ds(base + c * COLS, COLS), :]
+            part = coef_s[2 * c + half, 0, s] * lines[pl.ds(base + c * COLS, COLS), :]
             line = part if line is None else line + part
         line = pltpu.roll(line, turn, axis=1)
         return tuple(acc[h] + jnp.where(lane == w - h * NY, line, 0.0) for h in range(2))
 
-    acc = lax.fori_loop(0, SLOTS, slot, (jnp.zeros((COLS, NY), f32),) * 2, unroll=16)
+    acc = (jnp.zeros((COLS, NY), f32),) * 2
+
+    def some_slots(half, acc):
+        for s in range(SLOTS // 2):
+            acc = slot(half, s, acc)
+        return acc
+
+    acc = lax.fori_loop(0, 2, some_slots, acc)
     for h in range(2):
         for half in range(2):
             rows[2 * h + half] = acc[h][half * 8 : half * 8 + 8]
@@ -445,8 +451,8 @@
             vmem(LZ, CX, NY), vmem(LZ, CX, NY), vmem(LZ, CX, NY), vmem(LZ, CX, NY),
             vmem(9 * LZ, CX, NY),
             pltpu.VMEM((1, SLOTS), jnp.int32), pltpu.VMEM((1, SLOTS), jnp.int32),
-            pltpu.SMEM((3, 1, SLOTS), f32), pltpu.SMEM((1, 1), jnp.int32),
-            pltpu.VMEM((8, SLOTS), jnp.int32), pltpu.SMEM((8, SLOTS), jnp.int32),
+            pltpu.SMEM((6, 1, SLOTS // 2), f32), pltpu.SMEM((1, 1), jnp.int32),
+            pltpu.VMEM((16, SLOTS // 2), jnp.int32), pltpu.SMEM((16, SLOTS // 2), jnp.int32),
             pltpu.VMEM((RES, WELLS), jnp.int32), vmem(2, 8, 256), vmem(8, 256),
             vmem(LZ * CX * PITCH, NY),
             vmem(4, 8, NY), vmem(8, 8, NY), vmem(32, 8, NY),
@@ -465,7 +471,7 @@
         ),
     )(
         rhs.reshape(BLOCKS, CX, NY), inv.reshape(9 * LZ, CX, NY), trans.reshape(3 * LZ, CX, NY),
-        cell, well, coef.transpose(1, 0, 2), count, node, net, resid.reshape(1, NET),
+        cell, well, coef.reshape(6, 1, SLOTS // 2), count, node, net, resid.reshape(1, NET),
     )
     return corr.reshape(1, 3, LZ, CX, NY), schur
 

time: 51.8 us -> 50.1 us (0.967)
  Pallas kernels: 49 us -> 47.3 us
    pallas_call x1, Pallas kernels: 49 us -> 47.3 us  [local(): pl.pallas_call(kernel, out_shape=(vmem(3 * LZ, CX, NY), vmem(COLS, NET)),...]
where the time goes in v4:
time: 50.1 us; the launch traced here: 50 us
  Pallas kernels  47.3 us (94%)
  local copies, waits for them, and re-layouts  1.4 us (3%)
  between operations  1.29 us (3%)
    pallas_call x1, Pallas kernels, local(): pl.pallas_call(kernel, out_shape=(vmem(3 * LZ, CX, NY), vmem(COLS, NET)),...  47.3 us
    unnamed x2, local copies, waits for them, and re-layouts  1.4 us

profile of v4, /device:TPU:1, one launch (start us, length us, event | category | flops | bytes accessed | tf_op | source)
XLA Modules:
  0.0 50.0 jit_solution(17966571088037393258)
XLA Ops:
  1.3 47.3 %shard_map.113 = (f32[24,32,128]{2,1,0:T(8,128)S(1)}, f32[16,2048]{1,0:T(8,128)S(1)}) custom-call(f32[384,32,128]{2,1,0:T(8,128)} %bitcast.7, f32[72,32,128]{2,1,0:T(8,128)} %bitcast.8, f32[24,32,128]{2,1,0:T(8,128)} %bitcast.9, s32[1,256]{1,0:T(1,128)} %cell.1, s32[1,256]{1,0:T(1,128)} %well.1, f32[6,1,128]{2,1,0:T(1,128)} %bitcast.11, ...), custom_call_target="tpu_custom_call" | custom-call | flops 120000000 | bytes 8500000 | tf_op jit(solution)/shard_map/pallas_call | solution.py:442
  48.6 0.7 %copy.14 = f32[1,3,8,32,128]{4,3,2,1,0:T(8,128)} copy(f32[1,3,8,32,128]{4,3,2,1,0:T(8,128)S(1)} %bitcast.6) | data formatting | bytes 786432
  49.3 0.7 %copy.15 = f32[16,2048]{1,0:T(8,128)} copy(f32[16,2048]{1,0:T(8,128)S(1)} %get-tuple-element.7) | data formatting | bytes 262144

commit v5 on v4

--- a/solution.py
+++ b/solution.py
@@ -282,13 +282,20 @@
                 for xt in columns:
                     tile(src, dst, g, l, xt, l > 0, l < LZ - 1, last)
 
+        if k == 0:
+
+            @pl.loop(0, GROUPS)
+            def _(g):
+                part(g, range(1, CX // 8 - 1))
+
         @pl.loop(0, GROUPS)
         def _(g):
+            if k:
+                part(g, range(1, CX // 8 - 1))
             halo_wait(src, k, g)
             part(g, (0, CX // 8 - 1))
             if not last:
                 halo_start(dst, k + 1, g)
-            part(g, range(1, CX // 8 - 1))
 
     panel = chain[SWEEPS]
 

time: 50.1 us -> 50.5 us (level)
  no operation moved by 1% of the time
where the time goes in v5:
time: 50.5 us; the launch traced here: 50.4 us
  Pallas kernels  47.7 us (94%)
  local copies, waits for them, and re-layouts  1.4 us (3%)
  between operations  1.29 us (3%)
    pallas_call x1, Pallas kernels, local(): pl.pallas_call(kernel, out_shape=(vmem(3 * LZ, CX, NY), vmem(COLS, NET)),...  47.7 us
    unnamed x2, local copies, waits for them, and re-layouts  1.4 us

profile of v5, /device:TPU:1, one launch (start us, length us, event | category | flops | bytes accessed | tf_op | source)
XLA Modules:
  0.0 50.4 jit_solution(3854948111306865003)
XLA Ops:
  1.3 47.7 %shard_map.113 = (f32[24,32,128]{2,1,0:T(8,128)S(1)}, f32[16,2048]{1,0:T(8,128)S(1)}) custom-call(f32[384,32,128]{2,1,0:T(8,128)} %bitcast.7, f32[72,32,128]{2,1,0:T(8,128)} %bitcast.8, f32[24,32,128]{2,1,0:T(8,128)} %bitcast.9, s32[1,256]{1,0:T(1,128)} %cell.1, s32[1,256]{1,0:T(1,128)} %well.1, f32[6,1,128]{2,1,0:T(1,128)} %bitcast.11, ...), custom_call_target="tpu_custom_call" | custom-call | flops 120000000 | bytes 8500000 | tf_op jit(solution)/shard_map/pallas_call | solution.py:449
  49.0 0.7 %copy.14 = f32[1,3,8,32,128]{4,3,2,1,0:T(8,128)} copy(f32[1,3,8,32,128]{4,3,2,1,0:T(8,128)S(1)} %bitcast.6) | data formatting | bytes 786432
  49.7 0.7 %copy.15 = f32[16,2048]{1,0:T(8,128)} copy(f32[16,2048]{1,0:T(8,128)S(1)} %get-tuple-element.7) | data formatting | bytes 262144
